TPU v7x, 256 devices: a whole 4x4x8 slice. The times are simulated.
256 devices in a mesh: row: 16 (over z, y_hi), col: 16 (over x, y_lo, core).
Axes of the slice: x: 4, y: 4 (y_hi: 2, y_lo: 2; y = y_hi * 2 + y_lo), z: 8, core: 2. Of those that a mesh axis runs over, the one named last changes fastest.
Arguments:
- grad_out: bfloat16 [16, 4096, 1024], P('row', 'col'), may hold values from -6 to 6
- preact: bfloat16 [16, 4096, 1024], P('row', 'col'), may hold values from -8 to 8
- features: bfloat16 [16, 4096, 1024], P('col', 'row'), may hold values from -6 to 6
- weight: bfloat16 [1024, 1024], replicated, may hold values from -0.1875 to 0.1875
- tile_values: bfloat16 [16, 16, 80, 128, 128], P('row', 'col'), may hold values from -0.125 to 0.125
- tile_row: int32 [16, 16, 80], P('row', 'col'), may hold values from 0 to 31, as said below
- tile_col: int32 [16, 16, 80], P('row', 'col'), may hold values from 0 to 31
- tile_count: int32 [16, 16], P('row', 'col'), may hold values from 1 to 80, as said below
Outputs:
- grad_in: bfloat16 [16, 4096, 1024], P('col', 'row')
- grad_weight: float32 [1024, 1024], replicated
Inputs may be any that keep to these rules, and one draw needn't show every extreme that they name: `tile_count`: some block uses all 80 slots. Within a block, the slots below its count name distinct (tile_row, tile_col) pairs; the other slots are ignored.
All inputs are finite; a program needn't handle non-finite values.
Results may differ from a plain program's by a relative error of at most 0.023.
Values may be sent and summed in bfloat16 or wider, within the bound.
No kernel may reach another device: no remote copies, remote signals or barrier semaphores. Data moves between devices by JAX's collectives and lax.ppermute only.
A program may use at most 128 MiB of HBM per device.

v0:
```python
import jax
import jax.numpy as jnp
from jax import lax
from jax.sharding import PartitionSpec as P


def silu_grad(grad_out, preact):
    pre_value = preact.astype(jnp.float32)
    sigmoid_val = jax.nn.sigmoid(pre_value)
    scaled = grad_out.astype(jnp.float32) * sigmoid_val * (1.0 + pre_value * (1.0 - sigmoid_val))
    return scaled.astype(jnp.bfloat16)


def tile_sum(panel, blocks, row_ids, col_ids, used_count, col_rows):
    tile_size = blocks.shape[1]
    width_feat = panel.shape[1]
    slot_total = blocks.shape[0]
    group_size = min(16, slot_total)
    step_count = -(-slot_total // group_size)
    live_mask = jnp.arange(step_count * group_size, dtype=jnp.int32) < used_count
    panel_tiles = panel.reshape(-1, tile_size, width_feat)

    def add_group(turn_index, total):
        offset = turn_index * group_size
        group_blocks = lax.dynamic_slice_in_dim(blocks, offset, group_size, 0)
        group_rows = lax.dynamic_slice_in_dim(row_ids, offset, group_size, 0)
        group_cols = lax.dynamic_slice_in_dim(col_ids, offset, group_size, 0)
        group_live = lax.dynamic_slice_in_dim(live_mask, offset, group_size, 0)
        picked = panel_tiles[group_rows]
        product = jnp.einsum(
            "kab,kaf->kbf", group_blocks, picked, preferred_element_type=jnp.float32
        )
        product = jnp.where(group_live[:, None, None], product, 0.0)
        return total.at[group_cols].add(product)

    initial = jnp.zeros((col_rows // tile_size, tile_size, width_feat), jnp.float32)
    total = lax.fori_loop(0, step_count, add_group, initial)
    return total.reshape(col_rows, width_feat)


def per_device(grad_out, preact, features, weight, tile_values, tile_row, tile_col, tile_count):
    grad_pre = silu_grad(grad_out[0], preact[0])
    panel = lax.all_gather(grad_pre, "col", axis=0, tiled=True)
    col_rows = features.shape[1] * lax.axis_size("row")
    partial_sum = tile_sum(
        panel, tile_values[0, 0], tile_row[0, 0], tile_col[0, 0], tile_count[0, 0], col_rows
    )
    mixed = lax.psum_scatter(
        partial_sum.astype(jnp.bfloat16), "row", scatter_dimension=0, tiled=True
    )
    grad_in = lax.dot_general(
        mixed, weight, (((1,), (1,)), ((), ())), preferred_element_type=jnp.float32
    )
    grad_in = grad_in.astype(jnp.bfloat16)[None]
    local_weight = lax.dot_general(
        features[0], mixed, (((0,), (0,)), ((), ())), preferred_element_type=jnp.float32
    )
    grad_weight = lax.psum(local_weight, ("row", "col"))
    return (grad_in, grad_weight)


def solution(mesh):
    return jax.shard_map(
        per_device,
        mesh=mesh,
        in_specs=(
            P("row", "col", None),
            P("row", "col", None),
            P("col", "row", None),
            P(),
            P("row", "col", None, None, None),
            P("row", "col", None),
            P("row", "col", None),
            P("row", "col"),
        ),
        out_specs=(P("col", "row", None), P()),
        check_vma=False,
    )
```

profile of v0, /device:TPU:1, one launch (start us, length us, event | category | flops | bytes accessed | tf_op | source)
XLA Modules:
  0.0 750.5 jit_solution(1272788206765011504)
XLA Ops:
  7.2 0.0 copy-start
  7.2 0.0 all-gather.2.cloned.1.call-start
  7.2 2.6 fusion.8
  9.8 0.0 all-gather.2.cloned.1.call-update
  9.8 0.0 reduce-scatter.2.cloned.1.call-start
  10.5 4.4 copy.10
  14.9 54.4 %all-gather.2.cloned.1.call-done = bf16[4096,1024]{1,0:T(8,128)(2,1)} async-done(((bf16[256,1024]{1,0:T(8,128)(2,1)}), bf16[4096,1024]{1,0:T(8,128)(2,1)}) %all-gather.2.cloned.1.call-update) | async-done | bytes 8388624 | tf_op jit(solution)/shard_map/all_gather | solution.py:43
  69.3 0.0 copy-start.3
  69.3 0.0 copy-start.4
  69.3 7.9 %broadcast_in_dim.47 = f32[32,128,1024]{2,1,0:T(8,128)} broadcast(f32[]{:T(128)} %constant.45.clone.1), dimensions={} | broadcast | bytes 16777220 | tf_op jit(solution)/shard_map/broadcast_in_dim | solution.py:36
  77.2 0.0 copy-done.3
  77.2 0.0 copy-done.4
  77.2 156.9 %while.13 = (s32[]{:T(128)}, f32[32,128,1024]{2,1,0:T(8,128)}, s32[80]{0:T(128)S(1)}, pred[80]{0:T(512)(128)(4,1)S(1)}, bf16[80,128,128]{1,2,0:T(8,128)(2,1)}, /...) while((s32[]{:T(128)}, f32[32,128,1024]{2,1,0:T(8,128)}, ...), condition=%wide.region_2.3_spmd, body=%wide.region_0.2_spmd.sunk | while | flops 541066368 | bytes 46666392 | solution.py:37
  77.2 0.1 dynamic_slice.37
  77.3 0.1 compare_select_fusion.3
  77.4 6.2 gather_fusion
  83.6 6.8 broadcast_select_fusion.2
  90.4 18.4 %scatter_fusion = f32[32,128,1024]{2,1,0:T(8,128)} fusion(f32[32,128,1024]{2,1,0:T(8,128)} %get-tuple-element.204, s32[16]{0:T(128)S(1)} %get-tuple-element.190, f32[16,128,1024]{2,1,0:T(8,128)} %broadcast_select_fusion.2), kind=kCustom, calls=%fused_computation.1.clone.1 | custom fusion | flops 2097152 | bytes 25165888 | tf_op jit(solution)/shard_map/while/body/eval_jaxpr/scatter-add | solution.py:34
  108.8 0.1 dynamic_slice.37
  108.9 0.1 compare_select_fusion.3
  108.9 6.2 gather_fusion
  115.2 6.8 broadcast_select_fusion.2
  122.0 18.0 %scatter_fusion = f32[32,128,1024]{2,1,0:T(8,128)} fusion(f32[32,128,1024]{2,1,0:T(8,128)} %get-tuple-element.204, s32[16]{0:T(128)S(1)} %get-tuple-element.190, f32[16,128,1024]{2,1,0:T(8,128)} %broadcast_select_fusion.2), kind=kCustom, calls=%fused_computation.1.clone.1 | custom fusion | flops 2097152 | bytes 25165888 | tf_op jit(solution)/shard_map/while/body/eval_jaxpr/scatter-add | solution.py:34
  139.9 0.1 dynamic_slice.37
  140.0 0.1 compare_select_fusion.3
  140.1 6.2 gather_fusion
  146.3 6.8 broadcast_select_fusion.2
  153.1 18.4 %scatter_fusion = f32[32,128,1024]{2,1,0:T(8,128)} fusion(f32[32,128,1024]{2,1,0:T(8,128)} %get-tuple-element.204, s32[16]{0:T(128)S(1)} %get-tuple-element.190, f32[16,128,1024]{2,1,0:T(8,128)} %broadcast_select_fusion.2), kind=kCustom, calls=%fused_computation.1.clone.1 | custom fusion | flops 2097152 | bytes 25165888 | tf_op jit(solution)/shard_map/while/body/eval_jaxpr/scatter-add | solution.py:34
  171.5 0.1 dynamic_slice.37
  171.6 0.1 compare_select_fusion.3
  171.7 6.2 gather_fusion
  177.9 6.8 broadcast_select_fusion.2
  184.7 18.2 %scatter_fusion = f32[32,128,1024]{2,1,0:T(8,128)} fusion(f32[32,128,1024]{2,1,0:T(8,128)} %get-tuple-element.204, s32[16]{0:T(128)S(1)} %get-tuple-element.190, f32[16,128,1024]{2,1,0:T(8,128)} %broadcast_select_fusion.2), kind=kCustom, calls=%fused_computation.1.clone.1 | custom fusion | flops 2097152 | bytes 25165888 | tf_op jit(solution)/shard_map/while/body/eval_jaxpr/scatter-add | solution.py:34
  202.9 0.1 dynamic_slice.37
  202.9 0.1 compare_select_fusion.3
  203.0 6.2 gather_fusion
  209.2 6.8 broadcast_select_fusion.2
  216.0 18.1 %scatter_fusion = f32[32,128,1024]{2,1,0:T(8,128)} fusion(f32[32,128,1024]{2,1,0:T(8,128)} %get-tuple-element.204, s32[16]{0:T(128)S(1)} %get-tuple-element.190, f32[16,128,1024]{2,1,0:T(8,128)} %broadcast_select_fusion.2), kind=kCustom, calls=%fused_computation.1.clone.1 | custom fusion | flops 2097152 | bytes 25165888 | tf_op jit(solution)/shard_map/while/body/eval_jaxpr/scatter-add | solution.py:34
  234.2 9.1 %convert_element_type.29 = bf16[32,128,1024]{2,1,0:T(8,128)(2,1)} convert(f32[32,128,1024]{2,1,0:T(8,128)} %get-tuple-element.126) | non-fusion elementwise | flops 4194304 | bytes 25165824 | tf_op jit(solution)/shard_map/convert_element_type | solution.py:49
  243.3 0.0 copy-start.2
  243.3 0.0 reduce-scatter.2.cloned.1.call-update
  243.3 0.0 all-reduce.2.cloned.1.call-start
  243.4 219.8 %reduce-scatter.2.cloned.1.call-done = bf16[256,1024]{1,0:T(8,128)(2,1)} async-done(((bf16[4096,1024]{1,0:T(8,128)(2,1)}), bf16[256,1024]{1,0:T(8,128)(2,1)}) %reduce-scatter.2.cloned.1.call-update) | async-done | bytes 524304 | tf_op jit(solution)/shard_map/reduce_scatter | solution.py:48
  463.1 0.0 copy-done.2
  463.1 3.8 convolution_bitcast_fusion
  466.9 0.0 copy-start.1
  466.9 0.0 all-reduce.2.cloned.1.call-update
  467.0 0.0 copy-done
  467.0 1.0 copy-done.1
  468.0 1.5 fusion.2
  469.5 269.1 %all-reduce.2.cloned.1.call-done = f32[1024,1024]{0,1:T(8,128)} async-done(((f32[1024,1024]{0,1:T(8,128)}), f32[1024,1024]{0,1:T(8,128)}) %all-reduce.2.cloned.1.call-update) | async-done | bytes 4194320 | tf_op jit(solution)/shard_map/psum | solution.py:58
  738.6 5.3 copy.11
  (6 shorter events, 0.0 us)
Async XLA Ops:
  7.2 459.8 %copy-start = (bf16[1024,1024]{1,0:T(8,128)(2,1)S(1)}, bf16[1024,1024]{1,0:T(8,128)(2,1)}, u32[]{:S(2)}) copy-start(bf16[1024,1024]{1,0:T(8,128)(2,1)} %param.13) | copy-start | bytes 6291460
  7.2 62.2 %all-gather.2.cloned.1.call-start = ((), (), s32[]{:S(2)}) async-start(), calls=%async_computation.1 | async-start | bytes 8912896 | tf_op jit(solution)/shard_map/all_gather | solution.py:43
  9.8 453.3 %reduce-scatter.2.cloned.1.call-start = ((), (), s32[]{:S(2)}) async-start(), calls=%async_computation.2 | async-start | bytes 8912896 | tf_op jit(solution)/shard_map/reduce_scatter | solution.py:48
  69.3 7.9 %copy-start.3 = (s32[1,1,80]{2,1,0:T(1,128)S(1)}, s32[1,1,80]{2,1,0:T(1,128)}, u32[]{:S(2)}) copy-start(s32[1,1,80]{2,1,0:T(1,128)} %param.16) | copy-start | bytes 964
  69.3 7.9 %copy-start.4 = (s32[1,1,80]{2,1,0:T(1,128)S(1)}, s32[1,1,80]{2,1,0:T(1,128)}, u32[]{:S(2)}) copy-start(s32[1,1,80]{2,1,0:T(1,128)} %param.15) | copy-start | bytes 964
  243.3 219.9 %copy-start.2 = (bf16[1,256,1024]{2,1,0:T(8,128)(2,1)S(1)}, bf16[1,256,1024]{2,1,0:T(8,128)(2,1)}, u32[]{:S(2)}) copy-start(bf16[1,256,1024]{2,1,0:T(8,128)(2,1)} %param.12) | copy-start | bytes 1572868
  243.3 495.3 %all-reduce.2.cloned.1.call-start = ((), (), s32[]{:S(2)}) async-start(), calls=%async_computation.3 | async-start | bytes 8388608 | tf_op jit(solution)/shard_map/psum | solution.py:58
  466.9 1.0 copy-start.1
Sparse Core Ops, SparseCore 0:
  10.4 58.8 all-gather.1
  243.4 219.6 reduce-scatter.1
  469.2 269.4 all-reduce.1
where the time goes:
time: 752 us; the launch traced here: 751 us
  waiting for transfers between devices  543 us (72%)
  other arithmetic  103 us (14%)
  local copies, waits for them, and re-layouts  50.1 us (7%)
  matrix products  39.4 us (5%)
  between operations  14.4 us (2%)
    psum x1, waiting for transfers between devices, per_device(): grad_weight = lax.psum(local_weight, ('row', 'col'))  269 us
    reduce_scatter x1, waiting for transfers between devices, per_device(): lax.psum_scatter(partial_sum.astype(jnp.bfloat16), 'row', scatter_dimensi...  220 us
    scatter-add x5, other arithmetic, add_group(): return total.at[group_cols].add(product)  91 us
    all_gather x1, waiting for transfers between devices, per_device(): panel = lax.all_gather(grad_pre, 'col', axis=0, tiled=True)  54.4 us
    dot_general x5, matrix products, add_group(): jnp.einsum('kab,kaf->kbf', group_blocks, picked, preferred_element_type=j...  34.1 us
    gather x5, local copies, waits for them, and re-layouts, add_group(): picked = panel_tiles[group_rows]  31 us
  transfers between devices with their start and end apart: 3, of which 3 were waited for; matrix products, arithmetic and copies ran while one was open for 1% of the time, Pallas kernels for 0%

commit v1 on v0

v1 whole, which is shorter than its diff:
```python
import jax
import jax.numpy as jnp
from jax import lax
from jax.experimental import pallas as pl
from jax.experimental.pallas import tpu as pltpu
from jax.sharding import Mesh, PartitionSpec as P

ROW = ("z", "yh")
COL = ("x", "yl", "core")
CHUNKS = 4
GROUP = 8
PARTS = ((0, 1, 2), (3,))


def silu_grad(grad_out, preact):
    pre_value = preact.astype(jnp.float32)
    sigmoid_val = jax.nn.sigmoid(pre_value)
    scaled = grad_out.astype(jnp.float32) * sigmoid_val * (1.0 + pre_value * (1.0 - sigmoid_val))
    return scaled.astype(jnp.bfloat16)


def tile_kernel(count_ref, row_ref, col_ref, blocks_ref, panel_ref, out_ref, total):
    tiles, size, width = total.shape
    tiles = tiles - 1
    slots = blocks_ref.shape[0]
    count = count_ref[0]
    total[...] = jnp.zeros_like(total)

    def add_group(step, carry):
        products = []
        for u in range(GROUP):
            slot = step * GROUP + u
            start = pl.multiple_of(row_ref[slot] * size, size)
            products.append(lax.dot_general(
                blocks_ref[slot], panel_ref[pl.ds(start, size), :], (((0,), (0,)), ((), ())),
                preferred_element_type=jnp.float32,
            ))
        for u in range(GROUP):
            slot = step * GROUP + u
            place = jnp.where(slot < count, col_ref[slot], tiles)
            total[place] += products[u]
        return carry

    lax.fori_loop(0, (count + GROUP - 1) // GROUP, add_group, 0)

    def store(tile, carry):
        out_ref[tile] = total[tile].astype(out_ref.dtype)
        return carry

    lax.fori_loop(0, tiles, store, 0)


def tile_sum(panel, blocks, row_ids, col_ids, used_count, col_tiles):
    slots, size, _ = blocks.shape
    width = panel.shape[1]
    pad = -slots % GROUP
    if pad:
        blocks = jnp.pad(blocks, ((0, pad), (0, 0), (0, 0)))
        row_ids, col_ids = jnp.pad(row_ids, (0, pad)), jnp.pad(col_ids, (0, pad))
    return pl.pallas_call(
        tile_kernel,
        out_shape=jax.ShapeDtypeStruct((col_tiles, size, width), jnp.bfloat16),
        in_specs=[pl.BlockSpec(memory_space=pltpu.SMEM)] * 3 + [pl.BlockSpec(memory_space=pltpu.VMEM)] * 2,
        out_specs=pl.BlockSpec(memory_space=pltpu.VMEM),
        scratch_shapes=[pltpu.VMEM((col_tiles + 1, size, width), jnp.float32)],
        compiler_params=pltpu.CompilerParams(vmem_limit_bytes=40 * 2**20),
        cost_estimate=pl.CostEstimate(
            flops=2 * slots * size * size * width,
            bytes_accessed=2 * (blocks.size + panel.size + col_tiles * size * width),
            transcendentals=0,
        ),
    )(used_count, row_ids, col_ids, blocks, panel)


def row_sum(partial, ways):
    size = lax.axis_size("z")
    here = lax.axis_index("z")
    pieces = partial.reshape(size, -1, partial.shape[-1])

    def own(place):
        return lax.dynamic_index_in_dim(pieces, jnp.bitwise_and(place, size - 1), 0, keepdims=False)

    arrived = []
    for way, hops in ways:
        perm = [(i, (i + way) % size) for i in range(size)]
        moving = own(here + way * hops)
        for hop in range(hops, 0, -1):
            moving = lax.ppermute(moving, "z", perm)
            if hop > 1:
                moving = (moving.astype(jnp.float32) + own(here + way * (hop - 1)).astype(jnp.float32)).astype(jnp.bfloat16)
        arrived.append(moving)
    arrived.append(own(here))
    half = lax.axis_index("yh")

    def total(which):
        halves = [lax.dynamic_index_in_dim(t.reshape(2, -1, t.shape[-1]), which, 0, keepdims=False) for t in arrived]
        return sum(t.astype(jnp.float32) for t in halves)

    other = lax.ppermute(total(1 - half).astype(jnp.bfloat16), "yh", [(0, 1), (1, 0)])
    return (total(half) + other.astype(jnp.float32)).astype(jnp.bfloat16)


def sum_everywhere(terms):
    rows = lax.axis_size(ROW)
    cols = lax.axis_size(COL)
    cores = lax.axis_size("core")
    n = len(terms)
    stack = jnp.stack([t.astype(jnp.bfloat16) for t in terms])
    height, width = terms[0].shape
    size = (height * cores) // (rows * cols)
    lanes = width // cores
    stack = stack.reshape(n, rows, cols // cores, size, cores, lanes)
    stack = stack.transpose(2, 4, 1, 0, 3, 5).reshape(cols, rows, n, size, lanes)
    first = lax.all_to_all(stack, COL, 0, 0, tiled=True)
    first = jnp.sum(first.astype(jnp.float32), axis=0).astype(jnp.bfloat16)
    second = lax.all_to_all(first, ROW, 0, 0, tiled=True)
    second = jnp.sum(second.astype(jnp.float32), axis=0).astype(jnp.bfloat16)
    whole = lax.all_gather(second.reshape(n * size, lanes), COL, axis=0, tiled=True)
    whole = lax.all_gather(whole, ROW, axis=0, tiled=True)
    whole = whole.reshape(rows, cols // cores, cores, n, size, lanes)
    whole = whole.transpose(3, 0, 1, 4, 2, 5).reshape(n, height, width)
    return [whole[i].astype(jnp.float32) for i in range(n)]


def per_device(grad_out, preact, features, weight, tile_values, tile_row, tile_col, tile_count):
    width = grad_out.shape[-1] // CHUNKS
    col_tiles = features.shape[1] * lax.axis_size(ROW) // tile_values.shape[-1]
    mixed = []
    terms = []
    for c in range(CHUNKS):
        part = slice(c * width, (c + 1) * width)
        grad_pre = silu_grad(grad_out[0, :, part], preact[0, :, part])
        panel = lax.all_gather(grad_pre, COL, axis=0, tiled=True)
        partial = tile_sum(panel, tile_values[0, 0], tile_row[0, 0], tile_col[0, 0], tile_count[0], col_tiles)
        ways = ((1, 4), (-1, 3)) if c % 2 == 0 else ((1, 3), (-1, 4))
        mixed.append(row_sum(partial.reshape(-1, width), ways))
        terms.append(lax.dot_general(
            features[0], mixed[-1], (((0,), (0,)), ((), ())), preferred_element_type=jnp.float32
        ))
    grad_weight = []
    for members in PARTS:
        grad_weight += sum_everywhere([terms[c] for c in members])
    grad_in = lax.dot_general(
        jnp.concatenate(mixed, axis=1), weight, (((1,), (1,)), ((), ())), preferred_element_type=jnp.float32
    )
    return (grad_in.astype(jnp.bfloat16)[None], jnp.concatenate(grad_weight, axis=1))


def solution(mesh):
    devices = mesh.devices.reshape(8, 2, 4, 2, 2)
    fine = Mesh(devices, ROW + COL)
    return jax.shard_map(
        per_device,
        mesh=fine,
        in_specs=(
            P(ROW, COL, None),
            P(ROW, COL, None),
            P(COL, ROW, None),
            P(),
            P(ROW, COL, None, None, None),
            P(ROW, COL, None),
            P(ROW, COL, None),
            P(ROW, COL),
        ),
        out_specs=(P(COL, ROW, None), P()),
        check_vma=False,
    )
```

time: 752 us -> 399 us (0.53)
  waiting for transfers between devices: 543 us -> 155 us
  blocking collectives: 0 us -> 87 us
  other arithmetic: 103 us -> 29.2 us
  starting transfers between devices: 0.12 us -> 63.5 us
  matrix products: 39.4 us -> 2.84 us
  local copies, waits for them, and re-layouts: 50.1 us -> 28.4 us
  Pallas kernels: 0 us -> 11.3 us
    psum x1 -> x0, waiting for transfers between devices: 269 us -> none  [per_device(): grad_weight = lax.psum(local_weight, ('row', 'col'))]
    reduce_scatter x1 -> x0, waiting for transfers between devices: 220 us -> none  [per_device(): lax.psum_scatter(partial_sum.astype(jnp.bfloat16), 'row', scatter_dimensi...]
    scatter-add x5 -> x0, other arithmetic: 91 us -> none  [add_group(): return total.at[group_cols].add(product)]
    all_gather x0 -> x3, blocking collectives: none -> 71.6 us  [the longest x2 39.2 us: sum_everywhere(): lax.all_gather(second.reshape(n * size, lanes), COL, axis=0, tiled=True)]
    ppermute x0 -> x32, starting transfers between devices: none -> 47.6 us  [the longest x28 35.7 us: row_sum(): moving = lax.ppermute(moving, 'z', perm)]
    all_gather x1 -> x5, waiting for transfers between devices: 54.4 us -> 94.3 us  [the longest x4 94.3 us: per_device(): panel = lax.all_gather(grad_pre, COL, axis=0, tiled=True)]
    dot_general x7 -> x5, matrix products: 39.4 us -> 2.84 us  [the longest x1 1.57 us: per_device(): lax.dot_general(jnp.concatenate(mixed, axis=1), weight, (((1,), (1,)), ((...]
    ppermute x0 -> x32, waiting for transfers between devices: none -> 34.2 us  [the longest x28 29.6 us: row_sum(): moving = lax.ppermute(moving, 'z', perm)]
  transfers between devices with their start and end apart: 3 -> 40, of which waited for: 3 -> 14; matrix products, arithmetic and copies ran while one was open for 1% -> 9% of each run, Pallas kernels for 0% -> 3%
where the time goes in v1:
time: 399 us; the launch traced here: 392 us
  waiting for transfers between devices  155 us (39%)
  blocking collectives  87 us (22%)
  starting transfers between devices  63.5 us (16%)
  other arithmetic  29.2 us (7%)
  local copies, waits for them, and re-layouts  28.4 us (7%)
  between operations  14.9 us (4%)
  Pallas kernels  11.3 us (3%)
    all_gather x4, waiting for transfers between devices, per_device(): panel = lax.all_gather(grad_pre, COL, axis=0, tiled=True)  94.3 us
    all_gather x2, blocking collectives, sum_everywhere(): lax.all_gather(second.reshape(n * size, lanes), COL, axis=0, tiled=True)  39.2 us
    ppermute x28, starting transfers between devices, row_sum(): moving = lax.ppermute(moving, 'z', perm)  35.7 us
    all_gather x1, blocking collectives, sum_everywhere(): whole = lax.all_gather(whole, ROW, axis=0, tiled=True)  32.4 us
    ppermute x28, waiting for transfers between devices, row_sum(): moving = lax.ppermute(moving, 'z', perm)  29.6 us
    unnamed x50, local copies, waits for them, and re-layouts  19.3 us
    all_to_all x1, blocking collectives, sum_everywhere(): first = lax.all_to_all(stack, COL, 0, 0, tiled=True)  15.4 us
    all_to_all x2, waiting for transfers between devices, sum_everywhere(): second = lax.all_to_all(first, ROW, 0, 0, tiled=True)  12.8 us
  transfers between devices with their start and end apart: 40, of which 14 were waited for; matrix products, arithmetic and copies ran while one was open for 9% of the time, Pallas kernels for 3%

profile of v1, /device:TPU:1, one launch (start us, length us, event | category | flops | bytes accessed | tf_op | source)
XLA Modules:
  0.0 392.1 jit_solution(9344829410267913748)
XLA Ops:
  7.2 2.6 fusion.41
  12.6 38.6 %all-gather.6.cloned.1.call-done.panel_ref = bf16[4096,256]{1,0:T(8,128)(2,1)} async-done(((bf16[256,256]{1,0:T(8,128)(2,1)}), bf16[4096,256]{1,0:T(8,128)(2,1)}) %all-gather.6.cloned.1.call-update) | async-done | bytes 2097168 | tf_op jit(solution)/shard_map/all_gather | solution.py:133
  51.2 1.7 copy-done.1
  53.0 1.6 copy-done.13
  54.6 2.8 shard_map.95
  57.4 1.3 copy-done.7
  60.1 2.1 collective-permute-start.4
  62.2 28.0 %all-gather.8.cloned.1.call-done.panel_ref = bf16[4096,256]{1,0:T(8,128)(2,1)} async-done(((bf16[256,256]{1,0:T(8,128)(2,1)}), bf16[4096,256]{1,0:T(8,128)(2,1)}) %all-gather.8.cloned.1.call-update) | async-done | bytes 2097168 | tf_op jit(solution)/shard_map/all_gather | solution.py:133
  90.2 1.7 copy-done.2
  91.9 1.6 copy-done.12
  93.5 2.8 shard_map.96
  96.4 1.3 copy-done.5
  98.4 2.4 collective-permute-start.11
  100.8 27.7 %all-gather.10.cloned.1.call-done.panel_ref = bf16[4096,256]{1,0:T(8,128)(2,1)} async-done(((bf16[256,256]{1,0:T(8,128)(2,1)}), bf16[4096,256]{1,0:T(8,128)(2,1)}) %all-gather.10.cloned.1.call-update) | async-done | bytes 2097168 | tf_op jit(solution)/shard_map/all_gather | solution.py:133
  128.5 1.7 copy-done.3
  130.2 1.6 copy-done.11
  131.8 2.8 shard_map.97
  135.6 1.9 collective-permute-start.20
  139.7 4.4 %collective-permute-done.16 = bf16[512,256]{1,0:T(8,128)(2,1)S(1)} collective-permute-done((bf16[512,256]{1,0:T(8,128)(2,1)S(1)}, bf16[512,256]{1,0:T(8,128)(2,1)S(1)}, u32[]{:S(2)}, u32[]{:S(2)}) %collective-permute-start.16) | collective-permute-done | bytes 262176 | tf_op jit(solution)/shard_map/ppermute | solution.py:88
  145.7 4.0 %collective-permute-done.1 = bf16[512,256]{1,0:T(8,128)(2,1)S(1)} collective-permute-done((bf16[512,256]{1,0:T(8,128)(2,1)S(1)}, bf16[512,256]{1,0:T(8,128)(2,1)S(1)}, u32[]{:S(2)}, u32[]{:S(2)}) %collective-permute-start.1) | collective-permute-done | bytes 262176 | tf_op jit(solution)/shard_map/ppermute | solution.py:88
  150.9 2.7 collective-permute-start.5
  155.1 1.2 collective-permute-start.9
  157.6 2.9 collective-permute-done.2
  160.4 2.2 collective-permute-start.21
  163.5 3.3 collective-permute-start.6
  167.8 1.2 collective-permute-start.10
  169.0 2.6 collective-permute-done.18
  171.7 2.3 collective-permute-start.14
  174.9 2.5 collective-permute-done.3
  177.4 2.2 collective-permute-start.22
  180.6 3.1 collective-permute-start.7
  183.8 1.7 fusion.65
  185.5 4.1 %collective-permute-start.15 = (bf16[256,256]{1,0:T(8,128)(2,1)}, bf16[256,256]{1,0:T(8,128)(2,1)}, u32[]{:S(2)}, u32[]{:S(2)}) collective-permute-start(bf16[256,256]{1,0:T(8,128)(2,1)} %fusion.65), channel_id=1, source_target_pairs={{0,16},{16,0},{1,17},{17,1},{2,18},{18,2},{3,19},{19,3},{4,20},{20... | collective-permute-start | bytes 393224 | tf_op jit(solution)/shard_map/ppermute | solution.py:99
  189.6 1.7 fusion.66
  191.2 3.9 collective-permute-start.23
  203.7 1.5 maximum_bitcast_fusion
  205.3 1.6 copy.26
  206.9 5.0 %all-to-all-start = ((bf16[16,16,3,8,128]{4,3,2,1,0:T(8,128)(2,1)}), bf16[16,16,3,8,128]{4,3,2,1,0:T(8,128)(2,1)}, u32[]{:S(2)}, u32[]{:S(2)}) async-start(bf16[16,16,3,8,128]{4,3,2,1,0:T(8,128)(2,1)} %bitcast.224), calls=%async_computation | async-start | bytes 3145728 | tf_op jit(solution)/shard_map/all_to_all | solution.py:114
  211.9 1.7 copy-done.4
  213.6 1.6 copy-done.10
  215.2 2.8 shard_map.98
  218.0 1.3 copy-done.9
  220.3 1.2 collective-permute-start.24
  221.6 11.8 %all-to-all-done = bf16[16,16,3,8,128]{4,3,2,1,0:T(8,128)(2,1)} async-done(((bf16[16,16,3,8,128]{4,3,2,1,0:T(8,128)(2,1)}), bf16[16,16,3,8,128]{4,3,2,1,0:T(8,128)(2,1)}, u32[]{:S(2)}, u32[]{:S(2)}) %all-to-all-start) | async-done | bytes 1572896 | tf_op jit(solution)/shard_map/all_to_all | solution.py:114
  233.3 2.3 reduce_sum.50
  235.6 6.3 %all-to-all-start.1 = ((bf16[16,3,8,128]{3,2,1,0:T(8,128)(2,1)}), bf16[16,3,8,128]{3,2,1,0:T(8,128)(2,1)S(1)}, u32[]{:S(2)}, u32[]{:S(2)}) async-start(bf16[16,3,8,128]{3,2,1,0:T(8,128)(2,1)} %reduce_sum.50), calls=%async_computation.1 | async-start | bytes 196608 | tf_op jit(solution)/shard_map/all_to_all | solution.py:116
  242.0 1.8 fusion.14
  243.8 2.6 collective-permute-start.28
  246.4 5.3 %all-to-all-done.1 = bf16[16,3,8,128]{3,2,1,0:T(8,128)(2,1)S(1)} async-done(((bf16[16,3,8,128]{3,2,1,0:T(8,128)(2,1)}), bf16[16,3,8,128]{3,2,1,0:T(8,128)(2,1)S(1)}, u32[]{:S(2)}, u32[]{:S(2)}) %all-to-all-start.1) | async-done | bytes 98336 | tf_op jit(solution)/shard_map/all_to_all | solution.py:116
  251.7 20.3 %all_gather.28 = bf16[384,128]{1,0:T(8,128)(2,1)} all-gather(bf16[24,128]{1,0:T(8,128)(2,1)S(1)} %bitcast.246), channel_id=1, replica_groups=mesh['z'=8,'yh'=2,'x'=4,'yl'=2,'core'=2] {'x','yl','core'}, dimensions={0}, use_global_device_ids=true | all-gather | bytes 104448 | tf_op jit(solution)/shard_map/all_gather | solution.py:118
  272.0 1.3 fusion.16
  273.7 2.4 collective-permute-start.29
  276.1 6.8 %collective-permute-done.25 = bf16[512,256]{1,0:T(8,128)(2,1)S(1)} collective-permute-done((bf16[512,256]{1,0:T(8,128)(2,1)S(1)}, bf16[512,256]{1,0:T(8,128)(2,1)S(1)}, u32[]{:S(2)}, u32[]{:S(2)}) %collective-permute-start.25) | collective-permute-done | bytes 262176 | tf_op jit(solution)/shard_map/ppermute | solution.py:88
  284.2 2.7 collective-permute-start.30
  286.9 6.4 %collective-permute-done.26 = bf16[512,256]{1,0:T(8,128)(2,1)S(1)} collective-permute-done((bf16[512,256]{1,0:T(8,128)(2,1)S(1)}, bf16[512,256]{1,0:T(8,128)(2,1)S(1)}, u32[]{:S(2)}, u32[]{:S(2)}) %collective-permute-start.26) | collective-permute-done | bytes 262176 | tf_op jit(solution)/shard_map/ppermute | solution.py:88
  294.1 4.6 %collective-permute-done.31 = bf16[256,256]{1,0:T(8,128)(2,1)S(1)} collective-permute-done((bf16[256,256]{1,0:T(8,128)(2,1)S(1)}, bf16[256,256]{1,0:T(8,128)(2,1)S(1)}, u32[]{:S(2)}, u32[]{:S(2)}) %collective-permute-start.31) | collective-permute-done | bytes 131104 | tf_op jit(solution)/shard_map/ppermute | solution.py:99
  300.2 15.4 %all_to_all.20 = bf16[16,16,1,8,128]{4,3,1,2,0:T(8,128)(2,1)S(1)} all-to-all(bf16[16,16,1,8,128]{4,3,1,2,0:T(8,128)(2,1)S(1)} %copy.29), channel_id=1, replica_groups=mesh['z'=8,'yh'=2,'x'=4,'yl'=2,'core'=2] {'x','yl','core'}, dimensions={0} | all-to-all | bytes 1048576 | tf_op jit(solution)/shard_map/all_to_all | solution.py:114
  316.2 4.4 %all-to-all-start.3 = ((bf16[16,1,8,128]{3,2,1,0:T(8,128)(2,1)}), bf16[16,1,8,128]{3,2,1,0:T(8,128)(2,1)S(1)}, u32[]{:S(2)}, u32[]{:S(2)}) async-start(bf16[16,1,8,128]{3,2,1,0:T(8,128)(2,1)} %bitcast.89), calls=%async_computation.3 | async-start | bytes 65536 | tf_op jit(solution)/shard_map/all_to_all | solution.py:116
  320.7 1.6 fusion
  322.2 7.5 %all-to-all-done.3 = bf16[16,1,8,128]{3,2,1,0:T(8,128)(2,1)S(1)} async-done(((bf16[16,1,8,128]{3,2,1,0:T(8,128)(2,1)}), bf16[16,1,8,128]{3,2,1,0:T(8,128)(2,1)S(1)}, u32[]{:S(2)}, u32[]{:S(2)}) %all-to-all-start.3) | async-done | bytes 32800 | tf_op jit(solution)/shard_map/all_to_all | solution.py:116
  329.8 18.9 %all_gather.30 = bf16[128,128]{1,0:T(8,128)(2,1)S(1)} all-gather(bf16[8,128]{1,0:T(8,128)(2,1)S(1)} %reduce_sum.54), channel_id=1, replica_groups=mesh['z'=8,'yh'=2,'x'=4,'yl'=2,'core'=2] {'x','yl','core'}, dimensions={0}, use_global_device_ids=true | all-gather | bytes 34816 | tf_op jit(solution)/shard_map/all_gather | solution.py:118
  348.7 32.4 %all_gather.31 = bf16[2048,128]{1,0:T(8,128)(2,1)S(1)} all-gather(bf16[128,128]{1,0:T(8,128)(2,1)S(1)} %all_gather.30), channel_id=1, replica_groups=mesh['z'=8,'yh'=2,'x'=4,'yl'=2,'core'=2] {'z','yh'}, dimensions={0}, use_global_device_ids=true | all-gather | bytes 557056 | tf_op jit(solution)/shard_map/all_gather | solution.py:119
  381.1 1.8 fusion.69
  383.0 2.6 maximum_convert_fusion
  (122 shorter events, 31.0 us)
Async XLA Ops:
  7.2 313.5 %copy-start = (bf16[1024,1024]{1,0:T(8,128)(2,1)S(1)}, bf16[1024,1024]{1,0:T(8,128)(2,1)}, u32[]{:S(2)}) copy-start(bf16[1024,1024]{1,0:T(8,128)(2,1)} %param.11) | copy-start | bytes 6291460
  7.2 44.1 %copy-start.14 = (s32[1,1,80]{2,1,0:T(1,128)S(1)}, s32[1,1,80]{2,1,0:T(1,128)}, u32[]{:S(2)}) copy-start(s32[1,1,80]{2,1,0:T(1,128)} %param.13) | copy-start | bytes 964
  7.2 44.1 %copy-start.15 = (s32[1,1,80]{2,1,0:T(1,128)S(1)}, s32[1,1,80]{2,1,0:T(1,128)}, u32[]{:S(2)}) copy-start(s32[1,1,80]{2,1,0:T(1,128)} %param.14) | copy-start | bytes 964
  7.2 44.0 %all-gather.6.cloned.1.call-start = ((), (), s32[]{:S(2)}) async-start(), calls=%async_computation.4 | async-start | bytes 2228224 | tf_op jit(solution)/shard_map/all_gather | solution.py:133
  9.9 80.3 %all-gather.8.cloned.1.call-start = ((), (), s32[]{:S(2)}) async-start(), calls=%async_computation.5 | async-start | bytes 2228224 | tf_op jit(solution)/shard_map/all_gather | solution.py:133
  10.6 117.8 %all-gather.10.cloned.1.call-start = ((), (), s32[]{:S(2)}) async-start(), calls=%async_computation.6 | async-start | bytes 2228224 | tf_op jit(solution)/shard_map/all_gather | solution.py:133
  11.4 200.5 %all-gather.12.cloned.1.call-start = ((), (), s32[]{:S(2)}) async-start(), calls=%async_computation.7 | async-start | bytes 2228224 | tf_op jit(solution)/shard_map/all_gather | solution.py:133
  51.2 1.7 copy-start.1
  53.0 1.6 copy-start.13
  57.4 1.4 copy-start.7
  59.5 76.1 %collective-permute-start = (bf16[512,256]{1,0:T(8,128)(2,1)}, bf16[512,256]{1,0:T(8,128)(2,1)}, u32[]{:S(2)}, u32[]{:S(2)}) collective-permute-start(bf16[512,256]{1,0:T(8,128)(2,1)} %get-tuple-element.6), channel_id=1, source_target_pairs={{0,32},{32,64},{64,96},{96,128},{128,160},{160,192},{192,224},{224... | collective-permute-start | bytes 786440 | tf_op jit(solution)/shard_map/ppermute | solution.py:88
  60.1 84.9 %collective-permute-start.4 = (bf16[512,256]{1,0:T(8,128)(2,1)S(1)}, bf16[512,256]{1,0:T(8,128)(2,1)}, u32[]{:S(2)}, u32[]{:S(2)}) collective-permute-start(bf16[512,256]{1,0:T(8,128)(2,1)S(1)} %get-tuple-element.8), channel_id=1, source_target_pairs={{0,224},{32,0},{64,32},{96,64},{128,96},{160,128},{192,160},{224,1... | collective-permute-start | bytes 786440 | tf_op jit(solution)/shard_map/ppermute | solution.py:88
  90.2 1.7 copy-start.2
  91.9 1.6 copy-start.12
  96.4 1.3 copy-start.5
  98.4 40.1 %collective-permute-start.11 = (bf16[512,256]{1,0:T(8,128)(2,1)}, bf16[512,256]{1,0:T(8,128)(2,1)}, u32[]{:S(2)}, u32[]{:S(2)}) collective-permute-start(bf16[512,256]{1,0:T(8,128)(2,1)} %get-tuple-element.15), channel_id=1, source_target_pairs={{0,224},{32,0},{64,32},{96,64},{128,96},{160,128},{192,160},{224,1... | collective-permute-start | bytes 786440 | tf_op jit(solution)/shard_map/ppermute | solution.py:88
  100.8 50.1 %collective-permute-start.8 = (bf16[512,256]{1,0:T(8,128)(2,1)S(1)}, bf16[512,256]{1,0:T(8,128)(2,1)}, u32[]{:S(2)}, u32[]{:S(2)}) collective-permute-start(bf16[512,256]{1,0:T(8,128)(2,1)S(1)} %get-tuple-element.13), channel_id=1, source_target_pairs={{0,32},{32,64},{64,96},{96,128},{128,160},{160,192},{192,224},{224... | collective-permute-start | bytes 786440 | tf_op jit(solution)/shard_map/ppermute | solution.py:88
  128.5 1.7 copy-start.3
  130.2 1.6 copy-start.11
  131.8 5.7 %copy-start.8 = (bf16[32,128,256]{2,1,0:T(8,128)(2,1)S(1)}, bf16[32,128,256]{2,1,0:T(8,128)(2,1)}, u32[]{:S(2)}) copy-start(bf16[32,128,256]{2,1,0:T(8,128)(2,1)} %copy-done.7) | copy-start | bytes 6291460
  134.6 4.0 %copy-start.6 = (bf16[32,128,256]{2,1,0:T(8,128)(2,1)S(1)}, bf16[32,128,256]{2,1,0:T(8,128)(2,1)}, u32[]{:S(2)}) copy-start(bf16[32,128,256]{2,1,0:T(8,128)(2,1)} %copy-done.5) | copy-start | bytes 6291460
  134.7 54.8 %copy-start.17 = (bf16[1,512,256]{2,1,0:T(8,128)(2,1)}, bf16[1,512,256]{2,1,0:T(8,128)(2,1)S(1)}, u32[]{:S(2)}) copy-start(bf16[1,512,256]{2,1,0:T(8,128)(2,1)S(1)} %get-tuple-element.21) | copy-start | bytes 786436
  134.7 9.3 %collective-permute-start.16 = (bf16[512,256]{1,0:T(8,128)(2,1)S(1)}, bf16[512,256]{1,0:T(8,128)(2,1)S(1)}, u32[]{:S(2)}, u32[]{:S(2)}) collective-permute-start(bf16[512,256]{1,0:T(8,128)(2,1)S(1)} %get-tuple-element.20), channel_id=1, source_target_pairs={{0,32},{32,64},{64,96},{96,128},{128,160},{160,192},{192,224},{224... | collective-permute-start | bytes 786440 | tf_op jit(solution)/shard_map/ppermute | solution.py:88
  135.6 19.5 %collective-permute-start.20 = (bf16[512,256]{1,0:T(8,128)(2,1)S(1)}, bf16[512,256]{1,0:T(8,128)(2,1)S(1)}, u32[]{:S(2)}, u32[]{:S(2)}) collective-permute-start(bf16[512,256]{1,0:T(8,128)(2,1)S(1)} %get-tuple-element.22), channel_id=1, source_target_pairs={{0,224},{32,0},{64,32},{96,64},{128,96},{160,128},{192,160},{224,1... | collective-permute-start | bytes 786440 | tf_op jit(solution)/shard_map/ppermute | solution.py:88
  138.5 11.1 %collective-permute-start.1 = (bf16[512,256]{1,0:T(8,128)(2,1)S(1)}, bf16[512,256]{1,0:T(8,128)(2,1)S(1)}, u32[]{:S(2)}, u32[]{:S(2)}) collective-permute-start(bf16[512,256]{1,0:T(8,128)(2,1)S(1)} %fusion.31), channel_id=1, source_target_pairs={{0,32},{32,64},{64,96},{96,128},{128,160},{160,192},{192,224},{224... | collective-permute-start | bytes 786440 | tf_op jit(solution)/shard_map/ppermute | solution.py:88
  144.0 9.5 %collective-permute-start.12 = (bf16[512,256]{1,0:T(8,128)(2,1)S(1)}, bf16[512,256]{1,0:T(8,128)(2,1)S(1)}, u32[]{:S(2)}, u32[]{:S(2)}) collective-permute-start(bf16[512,256]{1,0:T(8,128)(2,1)S(1)} %fusion.24), channel_id=1, source_target_pairs={{0,224},{32,0},{64,32},{96,64},{128,96},{160,128},{192,160},{224,1... | collective-permute-start | bytes 786440 | tf_op jit(solution)/shard_map/ppermute | solution.py:88
  145.0 11.4 %collective-permute-start.17 = (bf16[512,256]{1,0:T(8,128)(2,1)S(1)}, bf16[512,256]{1,0:T(8,128)(2,1)S(1)}, u32[]{:S(2)}, u32[]{:S(2)}) collective-permute-start(bf16[512,256]{1,0:T(8,128)(2,1)S(1)} %fusion.21), channel_id=1, source_target_pairs={{0,32},{32,64},{64,96},{96,128},{128,160},{160,192},{192,224},{224... | collective-permute-start | bytes 786440 | tf_op jit(solution)/shard_map/ppermute | solution.py:88
  150.8 9.7 %collective-permute-start.2 = (bf16[512,256]{1,0:T(8,128)(2,1)S(1)}, bf16[512,256]{1,0:T(8,128)(2,1)S(1)}, u32[]{:S(2)}, u32[]{:S(2)}) collective-permute-start(bf16[512,256]{1,0:T(8,128)(2,1)S(1)} %get-tuple-element.4), channel_id=1, source_target_pairs={{0,32},{32,64},{64,96},{96,128},{128,160},{160,192},{192,224},{224... | collective-permute-start | bytes 786440 | tf_op jit(solution)/shard_map/ppermute | solution.py:88
  150.9 11.8 %collective-permute-start.5 = (bf16[512,256]{1,0:T(8,128)(2,1)S(1)}, bf16[512,256]{1,0:T(8,128)(2,1)S(1)}, u32[]{:S(2)}, u32[]{:S(2)}) collective-permute-start(bf16[512,256]{1,0:T(8,128)(2,1)S(1)} %get-tuple-element.5), channel_id=1, source_target_pairs={{0,224},{32,0},{64,32},{96,64},{128,96},{160,128},{192,160},{224,1... | collective-permute-start | bytes 786440 | tf_op jit(solution)/shard_map/ppermute | solution.py:88
  154.6 8.9 %collective-permute-start.13 = (bf16[512,256]{1,0:T(8,128)(2,1)S(1)}, bf16[512,256]{1,0:T(8,128)(2,1)S(1)}, u32[]{:S(2)}, u32[]{:S(2)}) collective-permute-start(bf16[512,256]{1,0:T(8,128)(2,1)S(1)} %get-tuple-element.12), channel_id=1, source_target_pairs={{0,224},{32,0},{64,32},{96,64},{128,96},{160,128},{192,160},{224,1... | collective-permute-start | bytes 786440 | tf_op jit(solution)/shard_map/ppermute | solution.py:88
  155.1 11.7 %collective-permute-start.9 = (bf16[512,256]{1,0:T(8,128)(2,1)S(1)}, bf16[512,256]{1,0:T(8,128)(2,1)S(1)}, u32[]{:S(2)}, u32[]{:S(2)}) collective-permute-start(bf16[512,256]{1,0:T(8,128)(2,1)S(1)} %get-tuple-element.11), channel_id=1, source_target_pairs={{0,32},{32,64},{64,96},{96,128},{128,160},{160,192},{192,224},{224... | collective-permute-start | bytes 786440 | tf_op jit(solution)/shard_map/ppermute | solution.py:88
  156.5 15.1 %collective-permute-start.18 = (bf16[512,256]{1,0:T(8,128)(2,1)S(1)}, bf16[512,256]{1,0:T(8,128)(2,1)S(1)}, u32[]{:S(2)}, u32[]{:S(2)}) collective-permute-start(bf16[512,256]{1,0:T(8,128)(2,1)S(1)} %get-tuple-element.18), channel_id=1, source_target_pairs={{0,32},{32,64},{64,96},{96,128},{128,160},{160,192},{192,224},{224... | collective-permute-start | bytes 786440 | tf_op jit(solution)/shard_map/ppermute | solution.py:88
  160.4 13.5 %collective-permute-start.21 = (bf16[512,256]{1,0:T(8,128)(2,1)S(1)}, bf16[512,256]{1,0:T(8,128)(2,1)S(1)}, u32[]{:S(2)}, u32[]{:S(2)}) collective-permute-start(bf16[512,256]{1,0:T(8,128)(2,1)S(1)} %get-tuple-element.19), channel_id=1, source_target_pairs={{0,224},{32,0},{64,32},{96,64},{128,96},{160,128},{192,160},{224,1... | collective-permute-start | bytes 786440 | tf_op jit(solution)/shard_map/ppermute | solution.py:88
  163.5 13.9 %collective-permute-start.3 = (bf16[512,256]{1,0:T(8,128)(2,1)S(1)}, bf16[512,256]{1,0:T(8,128)(2,1)}, u32[]{:S(2)}, u32[]{:S(2)}) collective-permute-start(bf16[512,256]{1,0:T(8,128)(2,1)S(1)} %get-tuple-element.2), channel_id=1, source_target_pairs={{0,32},{32,64},{64,96},{96,128},{128,160},{160,192},{192,224},{224... | collective-permute-start | bytes 786440 | tf_op jit(solution)/shard_map/ppermute | solution.py:88
  163.5 16.1 %collective-permute-start.6 = (bf16[512,256]{1,0:T(8,128)(2,1)}, bf16[512,256]{1,0:T(8,128)(2,1)}, u32[]{:S(2)}, u32[]{:S(2)}) collective-permute-start(bf16[512,256]{1,0:T(8,128)(2,1)} %get-tuple-element.3), channel_id=1, source_target_pairs={{0,224},{32,0},{64,32},{96,64},{128,96},{160,128},{192,160},{224,1... | collective-permute-start | bytes 786440 | tf_op jit(solution)/shard_map/ppermute | solution.py:88
  167.8 28.4 %copy-start.16 = (bf16[1,256,1024]{2,1,0:T(8,128)(2,1)S(1)}, bf16[1,256,1024]{2,1,0:T(8,128)(2,1)}, u32[]{:S(2)}) copy-start(bf16[1,256,1024]{2,1,0:T(8,128)(2,1)} %param.10) | copy-start | bytes 1572868
  167.8 15.9 %collective-permute-start.10 = (bf16[512,256]{1,0:T(8,128)(2,1)}, bf16[512,256]{1,0:T(8,128)(2,1)}, u32[]{:S(2)}, u32[]{:S(2)}) collective-permute-start(bf16[512,256]{1,0:T(8,128)(2,1)} %get-tuple-element.9), channel_id=1, source_target_pairs={{0,32},{32,64},{64,96},{96,128},{128,160},{160,192},{192,224},{224... | collective-permute-start | bytes 786440 | tf_op jit(solution)/shard_map/ppermute | solution.py:88
  171.7 12.1 %collective-permute-start.14 = (bf16[512,256]{1,0:T(8,128)(2,1)}, bf16[512,256]{1,0:T(8,128)(2,1)}, u32[]{:S(2)}, u32[]{:S(2)}) collective-permute-start(bf16[512,256]{1,0:T(8,128)(2,1)} %get-tuple-element.10), channel_id=1, source_target_pairs={{0,224},{32,0},{64,32},{96,64},{128,96},{160,128},{192,160},{224,1... | collective-permute-start | bytes 786440 | tf_op jit(solution)/shard_map/ppermute | solution.py:88
  174.9 14.7 %collective-permute-start.19 = (bf16[512,256]{1,0:T(8,128)(2,1)}, bf16[512,256]{1,0:T(8,128)(2,1)}, u32[]{:S(2)}, u32[]{:S(2)}) collective-permute-start(bf16[512,256]{1,0:T(8,128)(2,1)} %get-tuple-element.16), channel_id=1, source_target_pairs={{0,32},{32,64},{64,96},{96,128},{128,160},{160,192},{192,224},{224... | collective-permute-start | bytes 786440 | tf_op jit(solution)/shard_map/ppermute | solution.py:88
  177.4 12.2 %collective-permute-start.22 = (bf16[512,256]{1,0:T(8,128)(2,1)}, bf16[512,256]{1,0:T(8,128)(2,1)}, u32[]{:S(2)}, u32[]{:S(2)}) collective-permute-start(bf16[512,256]{1,0:T(8,128)(2,1)} %get-tuple-element.17), channel_id=1, source_target_pairs={{0,224},{32,0},{64,32},{96,64},{128,96},{160,128},{192,160},{224,1... | collective-permute-start | bytes 786440 | tf_op jit(solution)/shard_map/ppermute | solution.py:88
  180.6 14.5 %collective-permute-start.7 = (bf16[256,256]{1,0:T(8,128)(2,1)S(1)}, bf16[256,256]{1,0:T(8,128)(2,1)S(1)}, u32[]{:S(2)}, u32[]{:S(2)}) collective-permute-start(bf16[256,256]{1,0:T(8,128)(2,1)S(1)} %fusion.64), channel_id=1, source_target_pairs={{0,16},{16,0},{1,17},{17,1},{2,18},{18,2},{3,19},{19,3},{4,20},{20... | collective-permute-start | bytes 393224 | tf_op jit(solution)/shard_map/ppermute | solution.py:99
  185.5 12.1 %collective-permute-start.15 = (bf16[256,256]{1,0:T(8,128)(2,1)}, bf16[256,256]{1,0:T(8,128)(2,1)}, u32[]{:S(2)}, u32[]{:S(2)}) collective-permute-start(bf16[256,256]{1,0:T(8,128)(2,1)} %fusion.65), channel_id=1, source_target_pairs={{0,16},{16,0},{1,17},{17,1},{2,18},{18,2},{3,19},{19,3},{4,20},{20... | collective-permute-start | bytes 393224 | tf_op jit(solution)/shard_map/ppermute | solution.py:99
  191.2 9.4 %collective-permute-start.23 = (bf16[256,256]{1,0:T(8,128)(2,1)}, bf16[256,256]{1,0:T(8,128)(2,1)}, u32[]{:S(2)}, u32[]{:S(2)}) collective-permute-start(bf16[256,256]{1,0:T(8,128)(2,1)} %fusion.66), channel_id=1, source_target_pairs={{0,16},{16,0},{1,17},{17,1},{2,18},{18,2},{3,19},{19,3},{4,20},{20... | collective-permute-start | bytes 393224 | tf_op jit(solution)/shard_map/ppermute | solution.py:99
  199.3 1.3 copy-start.18
  201.7 0.7 copy-start.21
  206.9 26.5 %all-to-all-start = ((bf16[16,16,3,8,128]{4,3,2,1,0:T(8,128)(2,1)}), bf16[16,16,3,8,128]{4,3,2,1,0:T(8,128)(2,1)}, u32[]{:S(2)}, u32[]{:S(2)}) async-start(bf16[16,16,3,8,128]{4,3,2,1,0:T(8,128)(2,1)} %bitcast.224), calls=%async_computation | async-start | bytes 3145728 | tf_op jit(solution)/shard_map/all_to_all | solution.py:114
  211.9 1.7 copy-start.4
  213.6 1.6 copy-start.10
  218.0 1.3 copy-start.9
  220.1 21.9 %collective-permute-start.27 = (bf16[512,256]{1,0:T(8,128)(2,1)}, bf16[512,256]{1,0:T(8,128)(2,1)}, u32[]{:S(2)}, u32[]{:S(2)}) collective-permute-start(bf16[512,256]{1,0:T(8,128)(2,1)} %get-tuple-element.29), channel_id=1, source_target_pairs={{0,224},{32,0},{64,32},{96,64},{128,96},{160,128},{192,160},{224,1... | collective-permute-start | bytes 786440 | tf_op jit(solution)/shard_map/ppermute | solution.py:88
  220.3 51.6 %collective-permute-start.24 = (bf16[512,256]{1,0:T(8,128)(2,1)S(1)}, bf16[512,256]{1,0:T(8,128)(2,1)}, u32[]{:S(2)}, u32[]{:S(2)}) collective-permute-start(bf16[512,256]{1,0:T(8,128)(2,1)S(1)} %get-tuple-element.27), channel_id=1, source_target_pairs={{0,32},{32,64},{64,96},{96,128},{128,160},{160,192},{192,224},{224... | collective-permute-start | bytes 786440 | tf_op jit(solution)/shard_map/ppermute | solution.py:88
  235.6 16.0 %all-to-all-start.1 = ((bf16[16,3,8,128]{3,2,1,0:T(8,128)(2,1)}), bf16[16,3,8,128]{3,2,1,0:T(8,128)(2,1)S(1)}, u32[]{:S(2)}, u32[]{:S(2)}) async-start(bf16[16,3,8,128]{3,2,1,0:T(8,128)(2,1)} %reduce_sum.50), calls=%async_computation.1 | async-start | bytes 196608 | tf_op jit(solution)/shard_map/all_to_all | solution.py:116
  242.0 139.1 %all-gather.14.cloned.1.call-start = ((), (), s32[]{:S(2)}) async-start(), calls=%async_computation.8 | async-start | bytes 1671168 | tf_op jit(solution)/shard_map/all_gather | solution.py:119
  243.8 28.2 %collective-permute-start.28 = (bf16[512,256]{1,0:T(8,128)(2,1)}, bf16[512,256]{1,0:T(8,128)(2,1)}, u32[]{:S(2)}, u32[]{:S(2)}) collective-permute-start(bf16[512,256]{1,0:T(8,128)(2,1)} %fusion.14), channel_id=1, source_target_pairs={{0,224},{32,0},{64,32},{96,64},{128,96},{160,128},{192,160},{224,1... | collective-permute-start | bytes 786440 | tf_op jit(solution)/shard_map/ppermute | solution.py:88
  273.3 9.6 %collective-permute-start.25 = (bf16[512,256]{1,0:T(8,128)(2,1)S(1)}, bf16[512,256]{1,0:T(8,128)(2,1)S(1)}, u32[]{:S(2)}, u32[]{:S(2)}) collective-permute-start(bf16[512,256]{1,0:T(8,128)(2,1)S(1)} %get-tuple-element.25), channel_id=1, source_target_pairs={{0,32},{32,64},{64,96},{96,128},{128,160},{160,192},{192,224},{224... | collective-permute-start | bytes 786440 | tf_op jit(solution)/shard_map/ppermute | solution.py:88
  273.7 9.2 %collective-permute-start.29 = (bf16[512,256]{1,0:T(8,128)(2,1)S(1)}, bf16[512,256]{1,0:T(8,128)(2,1)S(1)}, u32[]{:S(2)}, u32[]{:S(2)}) collective-permute-start(bf16[512,256]{1,0:T(8,128)(2,1)S(1)} %get-tuple-element.26), channel_id=1, source_target_pairs={{0,224},{32,0},{64,32},{96,64},{128,96},{160,128},{192,160},{224,1... | collective-permute-start | bytes 786440 | tf_op jit(solution)/shard_map/ppermute | solution.py:88
  284.1 9.1 %collective-permute-start.26 = (bf16[512,256]{1,0:T(8,128)(2,1)S(1)}, bf16[512,256]{1,0:T(8,128)(2,1)S(1)}, u32[]{:S(2)}, u32[]{:S(2)}) collective-permute-start(bf16[512,256]{1,0:T(8,128)(2,1)S(1)} %get-tuple-element.23), channel_id=1, source_target_pairs={{0,32},{32,64},{64,96},{96,128},{128,160},{160,192},{192,224},{224... | collective-permute-start | bytes 786440 | tf_op jit(solution)/shard_map/ppermute | solution.py:88
  284.2 9.1 %collective-permute-start.30 = (bf16[512,256]{1,0:T(8,128)(2,1)S(1)}, bf16[512,256]{1,0:T(8,128)(2,1)S(1)}, u32[]{:S(2)}, u32[]{:S(2)}) collective-permute-start(bf16[512,256]{1,0:T(8,128)(2,1)S(1)} %get-tuple-element.24), channel_id=1, source_target_pairs={{0,224},{32,0},{64,32},{96,64},{128,96},{160,128},{192,160},{224,1... | collective-permute-start | bytes 786440 | tf_op jit(solution)/shard_map/ppermute | solution.py:88
  293.3 5.4 %collective-permute-start.31 = (bf16[256,256]{1,0:T(8,128)(2,1)S(1)}, bf16[256,256]{1,0:T(8,128)(2,1)S(1)}, u32[]{:S(2)}, u32[]{:S(2)}) collective-permute-start(bf16[256,256]{1,0:T(8,128)(2,1)S(1)} %fusion.67), channel_id=1, source_target_pairs={{0,16},{16,0},{1,17},{17,1},{2,18},{18,2},{3,19},{19,3},{4,20},{20... | collective-permute-start | bytes 393224 | tf_op jit(solution)/shard_map/ppermute | solution.py:99
  298.8 0.7 copy-start.23
  299.8 20.9 %copy-start.20 = (bf16[256,256]{1,0:T(8,128)(2,1)S(1)}, bf16[256,256]{1,0:T(8,128)(2,1)}, u32[]{:S(2)}) copy-start(bf16[256,256]{1,0:T(8,128)(2,1)} %copy-done.19) | copy-start | bytes 393220
  299.8 20.9 %copy-start.22 = (bf16[256,256]{1,0:T(8,128)(2,1)S(1)}, bf16[256,256]{1,0:T(8,128)(2,1)}, u32[]{:S(2)}) copy-start(bf16[256,256]{1,0:T(8,128)(2,1)} %copy-done.21) | copy-start | bytes 393220
  300.0 20.7 %copy-start.24 = (bf16[256,256]{1,0:T(8,128)(2,1)S(1)}, bf16[256,256]{1,0:T(8,128)(2,1)}, u32[]{:S(2)}) copy-start(bf16[256,256]{1,0:T(8,128)(2,1)} %copy-done.23) | copy-start | bytes 393220
  316.2 13.5 %all-to-all-start.3 = ((bf16[16,1,8,128]{3,2,1,0:T(8,128)(2,1)}), bf16[16,1,8,128]{3,2,1,0:T(8,128)(2,1)S(1)}, u32[]{:S(2)}, u32[]{:S(2)}) async-start(bf16[16,1,8,128]{3,2,1,0:T(8,128)(2,1)} %bitcast.89), calls=%async_computation.3 | async-start | bytes 65536 | tf_op jit(solution)/shard_map/all_to_all | solution.py:116
  (1 other events, 0.7 us)
Sparse Core Ops, SparseCore 0:
  10.5 40.7 all-gather.5
  53.7 36.4 all-gather.7
  92.1 36.3 all-gather.9
  130.2 36.6 all-gather.11
  272.1 71.2 all-gather.13

commit v2 on v1

v2 whole, which is shorter than its diff:
```python
import functools

import jax
import jax.numpy as jnp
from jax import lax
from jax.experimental import pallas as pl
from jax.experimental.pallas import tpu as pltpu
from jax.sharding import Mesh, PartitionSpec as P

ROW = ("z", "yh")
COL = ("x", "yl", "core")
SIDE = ("yh", "x", "yl")
GROUP = 8
STEP = 256
CHUNKS = 2
REACH = 3


def silu_grad(grad_out, preact):
    pre_value = preact.astype(jnp.float32)
    sigmoid_val = jax.nn.sigmoid(pre_value)
    scaled = grad_out.astype(jnp.float32) * sigmoid_val * (1.0 + pre_value * (1.0 - sigmoid_val))
    return scaled.astype(jnp.bfloat16)


def tile_kernel(column, count_ref, row_ref, col_ref, blocks_hbm, panel_hbm, *rest):
    out_ref, total, blocks_ref, panel_ref, sems = rest[-5:]
    tiles, size, width = total.shape
    tiles = tiles - 1
    count = count_ref[0]
    copies = [
        pltpu.make_async_copy(blocks_hbm, blocks_ref, sems.at[0]),
        pltpu.make_async_copy(panel_hbm.at[:, pl.ds(column, width)], panel_ref, sems.at[1]),
    ]
    for copy in copies:
        copy.start()
    total[...] = jnp.zeros_like(total)
    for copy in copies:
        copy.wait()

    def add_group(step, carry):
        products = []
        for u in range(GROUP):
            slot = step * GROUP + u
            start = pl.multiple_of(row_ref[slot] * size, size)
            products.append(lax.dot_general(
                blocks_ref[slot], panel_ref[pl.ds(start, size), :], (((0,), (0,)), ((), ())),
                preferred_element_type=jnp.float32,
            ))
        for u in range(GROUP):
            slot = step * GROUP + u
            place = jnp.where(slot < count, col_ref[slot], tiles)
            total[place] += products[u]
        return carry

    lax.fori_loop(0, (count + GROUP - 1) // GROUP, add_group, 0)

    def store(tile, carry):
        out_ref[tile] = total[tile].astype(out_ref.dtype)
        return carry

    lax.fori_loop(0, tiles, store, 0)


def tile_sum(panel, column, width, blocks, row_ids, col_ids, used_count, col_tiles, after):
    slots, size, _ = blocks.shape
    depth = panel.shape[0]
    return pl.pallas_call(
        functools.partial(tile_kernel, column),
        out_shape=jax.ShapeDtypeStruct((col_tiles, size, width), jnp.bfloat16),
        in_specs=[pl.BlockSpec(memory_space=pltpu.SMEM)] * 3 + [pl.BlockSpec(memory_space=pltpu.HBM)] * 2
        + [pl.BlockSpec(memory_space=pl.ANY)] * len(after),
        out_specs=pl.BlockSpec(memory_space=pltpu.VMEM),
        scratch_shapes=[
            pltpu.VMEM((col_tiles + 1, size, width), jnp.float32),
            pltpu.VMEM(blocks.shape, jnp.bfloat16),
            pltpu.VMEM((depth, width), jnp.bfloat16),
            pltpu.SemaphoreType.DMA((2,)),
        ],
        compiler_params=pltpu.CompilerParams(vmem_limit_bytes=28 * 2**20),
        cost_estimate=pl.CostEstimate(
            flops=2 * slots * size * size * width,
            bytes_accessed=2 * (blocks.size + depth * width + col_tiles * size * width),
            transcendentals=0,
        ),
    )(used_count, row_ids, col_ids, blocks, panel, *after)


def shift(value, axis, way):
    size = lax.axis_size(axis)
    return lax.ppermute(value, axis, [(i, (i + way) % size) for i in range(size)])


def row_sum(partial, ways, reach):
    size = lax.axis_size("z")
    here = lax.axis_index("z")

    def own(place):
        return lax.dynamic_index_in_dim(partial, jnp.bitwise_and(place, size - 1), 0, keepdims=False)

    arrived = []
    passing = {}
    sent = {}
    for way, hops in ways:
        moving = own(here + way * hops)
        if hops == reach:
            passing[way * reach] = moving
        for hop in range(hops, 0, -1):
            sent.setdefault(hop, []).append(moving)
            moving = shift(moving, "z", way)
            if hop > 1:
                moving = (moving.astype(jnp.float32) + own(here + way * (hop - 1)).astype(jnp.float32)).astype(jnp.bfloat16)
            if hop == reach + 1:
                passing[way * reach] = moving
        arrived.append(moving)
    arrived.append(own(here))
    half = lax.axis_index("yh")

    def total(which):
        halves = [lax.dynamic_index_in_dim(t.reshape(2, -1, t.shape[-1]), which, 0, keepdims=False) for t in arrived]
        return sum(t.astype(jnp.float32) for t in halves)

    other = shift(total(1 - half).astype(jnp.bfloat16), "yh", 1)
    mixed = (total(half) + other.astype(jnp.float32)).astype(jnp.bfloat16)
    return mixed, passing, sent


def gather_features(turned, reach):
    found = []
    for start in (turned, shift(turned, "yh", 1)):
        near = {0: start}
        for k in range(1, reach + 1):
            near[k] = shift(near[k - 1], "z", -1)
            near[-k] = shift(near[1 - k], "z", 1)
        found.append(near)
    return found


def term_kernel(reach, place_ref, partial, below, above, *refs):
    distances = list(range(-reach, reach + 1))
    features = [dict(zip(distances, refs[:len(distances)])), dict(zip(distances, refs[len(distances):]))]
    out_ref, own, sems = refs[-3:]
    copies = []
    for i, k in enumerate(distances[1:-1]):
        place = jnp.bitwise_and(place_ref[0] + k, partial.shape[0] - 1)
        copies.append(pltpu.make_async_copy(partial.at[place], own.at[i], sems.at[i]))
    for copy in copies:
        copy.start()
    for copy in copies:
        copy.wait()
    depth = features[0][0].shape[1]

    def block(step, carry):
        rows = pl.ds(pl.multiple_of(step * STEP, STEP), STEP)
        total = jnp.zeros((STEP, out_ref.shape[1]), jnp.float32)
        for h in range(2):
            half = jnp.bitwise_xor(place_ref[1], h)
            at = pl.ds(pl.multiple_of(half * depth, depth), depth)
            for i, k in enumerate(distances):
                if k == -reach:
                    nodes = below[at, :]
                elif k == reach:
                    nodes = above[at, :]
                else:
                    nodes = own[i - 1, at, :]
                total += jnp.dot(features[h][k][rows, :], nodes, preferred_element_type=jnp.float32)
        out_ref[rows, :] = total.astype(out_ref.dtype)
        return carry

    lax.fori_loop(0, out_ref.shape[0] // STEP, block, 0)


def weight_terms(features, reach, partial, passing):
    distances = list(range(-reach, reach + 1))
    height = features[0][0].shape[0]
    rows, width = partial.shape[1:]
    vmem = pl.BlockSpec(memory_space=pltpu.VMEM)
    return pl.pallas_call(
        functools.partial(term_kernel, reach),
        out_shape=jax.ShapeDtypeStruct((height, width), jnp.bfloat16),
        in_specs=[pl.BlockSpec(memory_space=pltpu.SMEM), pl.BlockSpec(memory_space=pl.ANY)]
        + [vmem] * (2 + 2 * len(distances)),
        out_specs=vmem,
        scratch_shapes=[
            pltpu.VMEM((2 * reach - 1, rows, width), jnp.bfloat16),
            pltpu.SemaphoreType.DMA((2 * reach - 1,)),
        ],
        compiler_params=pltpu.CompilerParams(vmem_limit_bytes=28 * 2**20),
        cost_estimate=pl.CostEstimate(
            flops=2 * height * rows * width * len(distances),
            bytes_accessed=2 * (height * rows * len(distances) + (rows * len(distances) + height) * width),
            transcendentals=0,
        ),
    )(
        jnp.stack([lax.axis_index("z"), lax.axis_index("yh")]), partial, passing[-reach], passing[reach],
        *[near[k] for near in features for k in distances],
    )


def sum_everywhere(terms, sent):
    side = lax.axis_size(SIDE)
    depth = lax.axis_size("z")
    core = lax.axis_index("core")
    halves = []
    for term in terms:
        term = term.reshape(2, -1, term.shape[-1])
        mine = lax.dynamic_index_in_dim(term, core, 0, keepdims=False)
        other = shift(lax.dynamic_index_in_dim(term, 1 - core, 0, keepdims=False), "core", 1)
        halves.append((mine.astype(jnp.float32) + other.astype(jnp.float32)).astype(jnp.bfloat16))
    part = jnp.concatenate(halves, axis=1)
    part = lax.all_to_all(part.reshape(side, -1, part.shape[-1]), SIDE, 0, 0, tiled=True)
    part = jnp.sum(part.astype(jnp.float32), axis=0).astype(jnp.bfloat16)
    part, _ = lax.optimization_barrier((part, sent[2]))
    part = lax.all_to_all(jnp.broadcast_to(part[None], (depth,) + part.shape), "z", 0, 0, tiled=True)
    part = jnp.sum(part.astype(jnp.float32), axis=0).astype(jnp.bfloat16)
    part, _ = lax.optimization_barrier((part, sent[1]))
    half = lax.all_to_all(jnp.broadcast_to(part[None], (side,) + part.shape), SIDE, 0, 0, tiled=True)
    half = half.reshape(-1, half.shape[-1])
    other = shift(half, "core", 1)
    low = jnp.where(core == 0, half, other)
    high = jnp.where(core == 0, other, half)
    return jnp.concatenate([low, high]).astype(jnp.float32)


def per_device(grad_out, preact, features, weight, tile_values, tile_row, tile_col, tile_count):
    size = tile_values.shape[-1]
    width = grad_out.shape[-1] // CHUNKS
    col_tiles = features.shape[1] * lax.axis_size(ROW) // size
    tiles = (tile_values[0, 0], tile_row[0, 0], tile_col[0, 0], tile_count[0], col_tiles)

    panel = lax.all_gather(silu_grad(grad_out[0], preact[0]), COL, axis=0, tiled=True)
    own, other = gather_features(features[0].T, REACH)
    order = (
        [own[2], own[-2], other[1], other[-1]],
        [own[3], own[-3], other[2], other[-2]],
    )
    partials = []
    mixed = []
    terms = []
    sent = {}
    for c in range(CHUNKS):
        partial = tile_sum(panel, c * width, width, *tiles, order[c] + partials)
        partials.append(partial)
        partial = partial.reshape(lax.axis_size("z"), -1, width)
        ways = ((1, 4), (-1, 3)) if c % 2 == 0 else ((1, 3), (-1, 4))
        total, passing, moves = row_sum(partial, ways, REACH)
        for hop, sums in moves.items():
            sent.setdefault(hop, []).extend(sums)
        mixed.append(total)
        terms.append(weight_terms((own, other), REACH, partial, passing))
    grad_weight = sum_everywhere(terms, sent)
    grad_in = lax.dot_general(
        jnp.concatenate(mixed, axis=1), weight, (((1,), (1,)), ((), ())), preferred_element_type=jnp.float32
    )
    return (grad_in.astype(jnp.bfloat16)[None], grad_weight)


def solution(mesh):
    devices = mesh.devices.reshape(8, 2, 4, 2, 2)
    fine = Mesh(devices, ROW + COL)
    return jax.shard_map(
        per_device,
        mesh=fine,
        in_specs=(
            P(ROW, COL, None),
            P(ROW, COL, None),
            P(COL, ROW, None),
            P(),
            P(ROW, COL, None, None, None),
            P(ROW, COL, None),
            P(ROW, COL, None),
            P(ROW, COL),
        ),
        out_specs=(P(COL, ROW, None), P()),
        check_vma=False,
    )
```

time: 399 us -> 271 us (0.68)
  blocking collectives: 87 us -> 0 us
  waiting for transfers between devices: 155 us -> 95.7 us
  Pallas kernels: 11.3 us -> 21.9 us
  starting transfers between devices: 63.5 us -> 70.7 us
    all_gather x5 -> x1, waiting for transfers between devices: 94.3 us -> 17.4 us  [per_device(): lax.all_gather(silu_grad(grad_out[0], preact[0]), COL, axis=0, tiled=True)]
    all_gather x3 -> x0, blocking collectives: 71.6 us -> none  [the longest x2 39.2 us: sum_everywhere(): lax.all_gather(second.reshape(n * size, lanes), COL, axis=0, tiled=True)]
    ppermute x32, waiting for transfers between devices: 34.2 us -> 66.5 us  [shift(): lax.ppermute(value, axis, [(i, (i + way) % size) for i in range(size)])]
    all_to_all x1 -> x0, blocking collectives: 15.4 us -> none  [sum_everywhere(): first = lax.all_to_all(stack, COL, 0, 0, tiled=True)]
    all_to_all x3, waiting for transfers between devices: 24.6 us -> 11.7 us  [the longest x1 11.7 us: sum_everywhere(): lax.all_to_all(jnp.broadcast_to(part[None], (side,) + part.shape), SIDE,...]
    pallas_call x4, Pallas kernels: 11.3 us -> 21.9 us  [the longest x2 13.4 us: weight_terms(): pl.pallas_call(functools.partial(term_kernel, reach), out_shape=jax.Shape...]
    ppermute x32, starting transfers between devices: 47.6 us -> 52.8 us  [shift(): lax.ppermute(value, axis, [(i, (i + way) % size) for i in range(size)])]
    unnamed x50 -> x75, local copies, waits for them, and re-layouts: 19.3 us -> 23.9 us
  transfers between devices with their start and end apart: 40 -> 36, of which waited for: 14 -> 18; matrix products, arithmetic and copies ran while one was open for 9% -> 12% of each run, Pallas kernels for 3% -> 7%
where the time goes in v2:
time: 271 us; the launch traced here: 267 us
  waiting for transfers between devices  95.7 us (35%)
  starting transfers between devices  70.7 us (26%)
  local copies, waits for them, and re-layouts  31.2 us (12%)
  other arithmetic  30.6 us (11%)
  Pallas kernels  21.9 us (8%)
  between operations  15.1 us (6%)
    ppermute x32, waiting for transfers between devices, shift(): lax.ppermute(value, axis, [(i, (i + way) % size) for i in range(size)])  66.5 us
    ppermute x32, starting transfers between devices, shift(): lax.ppermute(value, axis, [(i, (i + way) % size) for i in range(size)])  52.8 us
    unnamed x75, local copies, waits for them, and re-layouts  23.9 us
    all_gather x1, waiting for transfers between devices, per_device(): lax.all_gather(silu_grad(grad_out[0], preact[0]), COL, axis=0, tiled=True)  17.4 us
    pallas_call x2, Pallas kernels, weight_terms(): pl.pallas_call(functools.partial(term_kernel, reach), out_shape=jax.Shape...  13.4 us
    convert_element_type x6, other arithmetic, row_sum(): (moving.astype(jnp.float32) + own(here + way * (hop - 1)).astype(jnp.floa...  12.5 us
    all_to_all x1, waiting for transfers between devices, sum_everywhere(): lax.all_to_all(jnp.broadcast_to(part[None], (side,) + part.shape), SIDE,...  11.7 us
    pallas_call x2, Pallas kernels, tile_sum(): pl.pallas_call(functools.partial(tile_kernel, column), out_shape=jax.Shap...  8.48 us
  transfers between devices with their start and end apart: 36, of which 18 were waited for; matrix products, arithmetic and copies ran while one was open for 12% of the time, Pallas kernels for 7%

profile of v2, /device:TPU:1, one launch (start us, length us, event | category | flops | bytes accessed | tf_op | source)
XLA Modules:
  0.0 266.7 jit_solution(60801275467834733)
XLA Ops:
  7.2 2.6 fusion.6
  9.8 1.2 copy.11
  11.1 6.5 %collective-permute-start = (bf16[1024,256]{1,0:T(8,128)(2,1)S(1)}, bf16[1024,256]{1,0:T(8,128)(2,1)S(1)}, u32[]{:S(2)}, u32[]{:S(2)}) collective-permute-start(bf16[1024,256]{1,0:T(8,128)(2,1)S(1)} %bitcast.110), channel_id=1, source_target_pairs={{0,224},{32,0},{64,32},{96,64},{128,96},{160,128},{192,160},{224,1... | collective-permute-start | bytes 1572872 | tf_op jit(solution)/shard_map/ppermute | solution.py:91
  17.6 2.9 %collective-permute-start.4 = (bf16[1024,256]{1,0:T(8,128)(2,1)S(1)}, bf16[1024,256]{1,0:T(8,128)(2,1)S(1)}, u32[]{:S(2)}, u32[]{:S(2)}) collective-permute-start(bf16[1024,256]{1,0:T(8,128)(2,1)S(1)} %bitcast.112), channel_id=1, source_target_pairs={{0,16},{16,0},{1,17},{17,1},{2,18},{18,2},{3,19},{19,3},{4,20},{20... | collective-permute-start | bytes 1572872 | tf_op jit(solution)/shard_map/ppermute | solution.py:91
  21.3 6.9 %collective-permute-done.refs_4_ = bf16[1024,256]{1,0:T(8,128)(2,1)S(1)} collective-permute-done((bf16[1024,256]{1,0:T(8,128)(2,1)S(1)}, bf16[1024,256]{1,0:T(8,128)(2,1)S(1)}, u32[]{:S(2)}, u32[]{:S(2)}) %collective-permute-start) | collective-permute-done | bytes 524320 | tf_op jit(solution)/shard_map/ppermute | solution.py:91
  28.1 3.4 %collective-permute-start.1 = (bf16[1024,256]{1,0:T(8,128)(2,1)S(1)}, bf16[1024,256]{1,0:T(8,128)(2,1)}, u32[]{:S(2)}, u32[]{:S(2)}) collective-permute-start(bf16[1024,256]{1,0:T(8,128)(2,1)S(1)} %collective-permute-done.refs_4_), channel_id=1, source_target_pairs={{0,224},{32,0},{64,32},{96,64},{128,96},{160,128},{192,160},{224,1... | collective-permute-start | bytes 1572872 | tf_op jit(solution)/shard_map/ppermute | solution.py:91
  33.2 2.0 collective-permute-done.4.refs_10_
  35.2 1.6 collective-permute-start.5
  37.6 3.6 %collective-permute-done.1.rest_0_.refs_5_ = bf16[1024,256]{1,0:T(8,128)(2,1)} collective-permute-done((bf16[1024,256]{1,0:T(8,128)(2,1)S(1)}, bf16[1024,256]{1,0:T(8,128)(2,1)}, u32[]{:S(2)}, u32[]{:S(2)}) %collective-permute-start.1) | collective-permute-done | bytes 524320 | tf_op jit(solution)/shard_map/ppermute | solution.py:91
  41.2 3.5 %collective-permute-start.15 = (bf16[1024,256]{1,0:T(8,128)(2,1)}, bf16[1024,256]{1,0:T(8,128)(2,1)S(1)}, u32[]{:S(2)}, u32[]{:S(2)}) collective-permute-start(bf16[1024,256]{1,0:T(8,128)(2,1)} %collective-permute-done.1.rest_0_.refs_5_), channel_id=1, source_target_pairs={{0,224},{32,0},{64,32},{96,64},{128,96},{160,128},{192,160},{224,1... | collective-permute-start | bytes 1572872 | tf_op jit(solution)/shard_map/ppermute | solution.py:91
  45.3 7.2 %collective-permute-done.5.rest_2_.refs_11_ = bf16[1024,256]{1,0:T(8,128)(2,1)} collective-permute-done((bf16[1024,256]{1,0:T(8,128)(2,1)S(1)}, bf16[1024,256]{1,0:T(8,128)(2,1)}, u32[]{:S(2)}, u32[]{:S(2)}) %collective-permute-start.5) | collective-permute-done | bytes 524320 | tf_op jit(solution)/shard_map/ppermute | solution.py:91
  52.5 3.5 %collective-permute-start.17 = (bf16[1024,256]{1,0:T(8,128)(2,1)}, bf16[1024,256]{1,0:T(8,128)(2,1)}, u32[]{:S(2)}, u32[]{:S(2)}) collective-permute-start(bf16[1024,256]{1,0:T(8,128)(2,1)} %collective-permute-done.5.rest_2_.refs_11_), channel_id=1, source_target_pairs={{0,224},{32,0},{64,32},{96,64},{128,96},{160,128},{192,160},{224,1... | collective-permute-start | bytes 1572872 | tf_op jit(solution)/shard_map/ppermute | solution.py:91
  57.2 17.4 %all-gather.2.cloned.1.call-done.panel_hbm = bf16[4096,1024]{1,0:T(8,128)(2,1)} async-done(((bf16[256,1024]{1,0:T(8,128)(2,1)}), bf16[4096,1024]{1,0:T(8,128)(2,1)}) %all-gather.2.cloned.1.call-update) | async-done | bytes 8388624 | tf_op jit(solution)/shard_map/all_gather | solution.py:231
  74.5 3.4 %copy-done.3 = bf16[4096,1024]{1,0:T(8,128)(2,1)S(1)} copy-done((bf16[4096,1024]{1,0:T(8,128)(2,1)S(1)}, bf16[4096,1024]{1,0:T(8,128)(2,1)}, u32[]{:S(2)}) %copy-start.3) | copy-done | bytes 8388632
  77.9 1.7 copy-done.6
  81.0 4.2 %shard_map.95.rest_4_ = bf16[32,128,512]{2,1,0:T(8,128)(2,1)S(1)} custom-call(s32[1]{0:T(128)} %bitcast.92.count_ref, s32[80]{0:T(128)S(1)} %bitcast.115, s32[80]{0:T(128)S(1)} %bitcast.117, bf16[80,128,128]{2,1,0:T(8,128)(2,1)S(1)} %bitcast.104, bf16[4096,1024]{1,0:T(8,128)(2,1)S(1)} %copy-done.3, bf16[1024,256]{1,0:T(8,128)(2,1)} %collective-permute-done.1.rest_0_.refs_5_, ...), custom_call_target="tpu_custom_call" | custom-call | flops 1342177280 | bytes 11010048 | tf_op jit(solution)/shard_map/pallas_call | solution.py:68
  85.3 4.2 %shard_map.96 = bf16[32,128,512]{2,1,0:T(8,128)(2,1)S(1)} custom-call(s32[1]{0:T(128)} %bitcast.93.count_ref, s32[80]{0:T(128)S(1)} %bitcast.116, s32[80]{0:T(128)S(1)} %bitcast.118, bf16[80,128,128]{2,1,0:T(8,128)(2,1)S(1)} %bitcast.105, bf16[4096,1024]{1,0:T(8,128)(2,1)S(1)} %copy-done.3, bf16[1024,256]{1,0:T(8,128)(2,1)S(1)} %collective-permute-done.15.rest_0_.refs_6_, ...), custom_call_target="tpu_custom_call" | custom-call | flops 1342177280 | bytes 11010048 | tf_op jit(solution)/shard_map/pallas_call | solution.py:68
  89.6 2.0 copy-done.4
  91.6 1.2 dynamic-slice_bitcast_fusion.3
  92.8 2.7 %collective-permute-start.22 = (bf16[512,512]{1,0:T(8,128)(2,1)}, bf16[512,512]{1,0:T(8,128)(2,1)}, u32[]{:S(2)}, u32[]{:S(2)}) collective-permute-start(bf16[512,512]{1,0:T(8,128)(2,1)} %get-tuple-element.19), channel_id=1, source_target_pairs={{0,224},{32,0},{64,32},{96,64},{128,96},{160,128},{192,160},{224,1... | collective-permute-start | bytes 1572872 | tf_op jit(solution)/shard_map/ppermute | solution.py:91
  95.5 5.0 %collective-permute-start.28 = (bf16[1024,256]{1,0:T(8,128)(2,1)}, bf16[1024,256]{1,0:T(8,128)(2,1)S(1)}, u32[]{:S(2)}, u32[]{:S(2)}) collective-permute-start(bf16[1024,256]{1,0:T(8,128)(2,1)} %collective-permute-done.17.rest_2_.refs_12_), channel_id=1, source_target_pairs={{0,224},{32,0},{64,32},{96,64},{128,96},{160,128},{192,160},{224,1... | collective-permute-start | bytes 1572872 | tf_op jit(solution)/shard_map/ppermute | solution.py:91
  100.6 2.4 dynamic-slice_bitcast_fusion.5
  103.1 3.3 %collective-permute-done.22 = bf16[512,512]{1,0:T(8,128)(2,1)} collective-permute-done((bf16[512,512]{1,0:T(8,128)(2,1)}, bf16[512,512]{1,0:T(8,128)(2,1)}, u32[]{:S(2)}, u32[]{:S(2)}) %collective-permute-start.22) | collective-permute-done | bytes 524320 | tf_op jit(solution)/shard_map/ppermute | solution.py:91
  106.4 1.3 fusion.11.below
  107.8 4.8 %collective-permute-done.27.refs_7_ = bf16[1024,256]{1,0:T(8,128)(2,1)S(1)} collective-permute-done((bf16[1024,256]{1,0:T(8,128)(2,1)}, bf16[1024,256]{1,0:T(8,128)(2,1)S(1)}, u32[]{:S(2)}, u32[]{:S(2)}) %collective-permute-start.27) | collective-permute-done | bytes 524320 | tf_op jit(solution)/shard_map/ppermute | solution.py:91
  113.4 4.2 %collective-permute-done.28.refs_13_ = bf16[1024,256]{1,0:T(8,128)(2,1)S(1)} collective-permute-done((bf16[1024,256]{1,0:T(8,128)(2,1)}, bf16[1024,256]{1,0:T(8,128)(2,1)S(1)}, u32[]{:S(2)}, u32[]{:S(2)}) %collective-permute-start.28) | collective-permute-done | bytes 524320 | tf_op jit(solution)/shard_map/ppermute | solution.py:91
  126.7 6.7 %shard_map.98 = bf16[1024,512]{1,0:T(8,128)(2,1)S(1)} custom-call(s32[2]{0:T(128)S(1)} %pad_add_fusion.place_ref, bf16[8,512,512]{2,1,0:T(8,128)(2,1)S(1)} %bitcast.103, bf16[512,512]{1,0:T(8,128)(2,1)S(1)} %fusion.11.below, bf16[512,512]{1,0:T(8,128)(2,1)S(1)} %copy-done.11, bf16[1024,256]{1,0:T(8,128)(2,1)S(1)} %copy-done.13, ...), custom_call_target="tpu_custom_call" | custom-call | flops 3758096384 | bytes 12058624 | tf_op jit(solution)/shard_map/pallas_call | solution.py:178
  134.2 1.7 collective-permute-start.30
  136.1 6.7 %shard_map.97 = bf16[1024,512]{1,0:T(8,128)(2,1)S(1)} custom-call(s32[2]{0:T(128)S(1)} %pad_add_fusion.place_ref, bf16[8,512,512]{2,1,0:T(8,128)(2,1)S(1)} %bitcast.98, bf16[512,512]{1,0:T(8,128)(2,1)S(1)} %get-tuple-element.12.below, bf16[512,512]{1,0:T(8,128)(2,1)S(1)} %fusion.18.above, bf16[1024,256]{1,0:T(8,128)(2,1)S(1)} %copy-done.14, ...), custom_call_target="tpu_custom_call" | custom-call | flops 3758096384 | bytes 12058624 | tf_op jit(solution)/shard_map/pallas_call | solution.py:178
  144.7 5.0 %collective-permute-start.23 = (bf16[512,512]{1,0:T(8,128)(2,1)}, bf16[512,512]{1,0:T(8,128)(2,1)}, u32[]{:S(2)}, u32[]{:S(2)}) collective-permute-start(bf16[512,512]{1,0:T(8,128)(2,1)} %copy-done.22), channel_id=1, source_target_pairs={{0,224},{32,0},{64,32},{96,64},{128,96},{160,128},{192,160},{224,1... | collective-permute-start | bytes 1572872 | tf_op jit(solution)/shard_map/ppermute | solution.py:91
  149.7 1.2 fusion.7
  150.9 1.4 fusion.8
  152.3 1.1 pad_maximum_fusion
  153.5 7.4 %all-to-all-start = ((bf16[16,32,1024]{2,1,0:T(8,128)(2,1)}), bf16[16,32,1024]{2,1,0:T(8,128)(2,1)}, u32[]{:S(2)}, u32[]{:S(2)}) async-start(bf16[16,32,1024]{2,1,0:T(8,128)(2,1)} %bitcast.120), calls=%async_computation | async-start | bytes 2097152 | tf_op jit(solution)/shard_map/all_to_all | solution.py:211
  160.8 1.5 collective-permute-start.11
  162.4 2.8 %fusion.13 = (bf16[512,512]{1,0:T(8,128)(2,1)}, bf16[512,512]{1,0:T(8,128)(2,1)}) fusion(bf16[512,512]{1,0:T(8,128)(2,1)} %collective-permute-done.19, bf16[8,512,512]{2,1,0:T(8,128)(2,1)} %bitcast.101, s32[]{:T(128)S(6)} %select_n.75, s32[]{:T(128)S(6)} %select_n.79, bf16[512,512]{1,0:T(8,128)(2,1)} %collective-permute-done.23), kind=kLoop, calls=%fused_computation.25 | loop fusion | flops 2097152 | bytes 3145736 | tf_op jit(solution)/shard_map/convert_element_type | solution.py:112
  165.9 2.0 collective-permute-start.24
  167.9 5.5 %collective-permute-done.11 = bf16[512,512]{1,0:T(8,128)(2,1)} collective-permute-done((bf16[512,512]{1,0:T(8,128)(2,1)S(1)}, bf16[512,512]{1,0:T(8,128)(2,1)}, u32[]{:S(2)}, u32[]{:S(2)}) %collective-permute-start.11) | collective-permute-done | bytes 524320 | tf_op jit(solution)/shard_map/ppermute | solution.py:91
  173.4 2.1 collective-permute-done.8
  175.5 2.6 fusion.17
  178.1 1.4 reduce_sum.24
  180.4 3.7 %all-to-all-start.1 = ((bf16[8,32,1024]{2,1,0:T(8,128)(2,1)}), bf16[8,32,1024]{2,1,0:T(8,128)(2,1)S(1)}, u32[]{:S(2)}, u32[]{:S(2)}) async-start(bf16[8,32,1024]{2,1,0:T(8,128)(2,1)} %broadcast_in_dim.7), calls=%async_computation.1 | async-start | bytes 1048576 | tf_op jit(solution)/shard_map/all_to_all | solution.py:214
  184.1 1.3 collective-permute-start.9
  185.4 1.5 collective-permute-start.12
  186.9 2.8 %fusion.12 = (bf16[512,512]{1,0:T(8,128)(2,1)}, bf16[512,512]{1,0:T(8,128)(2,1)}) fusion(bf16[512,512]{1,0:T(8,128)(2,1)} %collective-permute-done.20, bf16[8,512,512]{2,1,0:T(8,128)(2,1)} %bitcast.102, s32[]{:T(128)S(6)} %select_n.76, s32[]{:T(128)S(6)} %select_n.80, bf16[512,512]{1,0:T(8,128)(2,1)} %collective-permute-done.24), kind=kLoop, calls=%fused_computation.23 | loop fusion | flops 2097152 | bytes 3145736 | tf_op jit(solution)/shard_map/convert_element_type | solution.py:112
  189.7 19.4 %collective-permute-done.9 = bf16[512,512]{1,0:T(8,128)(2,1)} collective-permute-done((bf16[512,512]{1,0:T(8,128)(2,1)}, bf16[512,512]{1,0:T(8,128)(2,1)}, u32[]{:S(2)}, u32[]{:S(2)}) %collective-permute-start.9) | collective-permute-done | bytes 524320 | tf_op jit(solution)/shard_map/ppermute | solution.py:91
  209.1 2.8 %fusion.16 = (bf16[512,512]{1,0:T(8,128)(2,1)}, bf16[512,512]{1,0:T(8,128)(2,1)}) fusion(bf16[512,512]{1,0:T(8,128)(2,1)} %collective-permute-done.9, bf16[8,512,512]{2,1,0:T(8,128)(2,1)} %bitcast.96, s32[]{:T(128)S(6)} %select_n.76, s32[]{:T(128)S(6)} %select_n.80, bf16[512,512]{1,0:T(8,128)(2,1)} %collective-permute-done.12), kind=kLoop, calls=%fused_computation.31 | loop fusion | flops 2097152 | bytes 3145736 | tf_op jit(solution)/shard_map/convert_element_type | solution.py:112
  212.0 1.1 broadcast_in_dim.8
  213.1 6.8 %all-to-all-start.2 = ((bf16[16,32,1024]{2,1,0:T(8,128)(2,1)}), bf16[16,32,1024]{2,1,0:T(8,128)(2,1)S(1)}, u32[]{:S(2)}, u32[]{:S(2)}) async-start(bf16[16,32,1024]{2,1,0:T(8,128)(2,1)} %broadcast_in_dim.8), calls=%async_computation.2 | async-start | bytes 2097152 | tf_op jit(solution)/shard_map/all_to_all | solution.py:217
  219.9 1.5 collective-permute-start.21
  221.4 1.3 collective-permute-start.13
  222.8 11.7 %all-to-all-done.2 = bf16[16,32,1024]{2,1,0:T(8,128)(2,1)S(1)} async-done(((bf16[16,32,1024]{2,1,0:T(8,128)(2,1)}), bf16[16,32,1024]{2,1,0:T(8,128)(2,1)S(1)}, u32[]{:S(2)}, u32[]{:S(2)}) %all-to-all-start.2) | async-done | bytes 1048608 | tf_op jit(solution)/shard_map/all_to_all | solution.py:217
  234.6 3.9 %collective-permute-start.31 = (bf16[512,1024]{1,0:T(8,128)(2,1)S(1)}, bf16[512,1024]{1,0:T(8,128)(2,1)}, u32[]{:S(2)}, u32[]{:S(2)}) collective-permute-start(bf16[512,1024]{1,0:T(8,128)(2,1)S(1)} %bitcast.119), channel_id=1, source_target_pairs={{0,1},{1,0},{2,3},{3,2},{4,5},{5,4},{6,7},{7,6},{8,9},{9,8},{10,11... | collective-permute-start | bytes 3145736 | tf_op jit(solution)/shard_map/ppermute | solution.py:91
  238.5 1.9 fusion.25
  240.9 1.2 collective-permute-done.13
  243.1 1.9 fusion.24
  245.0 2.5 collective-permute-start.14
  247.5 1.4 collective-permute-done.26
  248.9 1.2 fusion.22
  250.2 2.9 %collective-permute-done.14 = bf16[256,512]{1,0:T(8,128)(2,1)} collective-permute-done((bf16[256,512]{1,0:T(8,128)(2,1)}, bf16[256,512]{1,0:T(8,128)(2,1)}, u32[]{:S(2)}, u32[]{:S(2)}) %collective-permute-start.14) | collective-permute-done | bytes 262176 | tf_op jit(solution)/shard_map/ppermute | solution.py:91
  253.1 1.3 fusion.23
  254.4 1.6 fusion
  256.0 1.4 broadcast_select_fusion.1
  257.4 2.4 maximum_convert_fusion
  (114 shorter events, 21.9 us)
Async XLA Ops:
  7.2 247.2 %copy-start = (bf16[1024,1024]{1,0:T(8,128)(2,1)S(1)}, bf16[1024,1024]{1,0:T(8,128)(2,1)}, u32[]{:S(2)}) copy-start(bf16[1024,1024]{1,0:T(8,128)(2,1)} %param.11) | copy-start | bytes 6291460
  7.2 67.3 %all-gather.2.cloned.1.call-start = ((), (), s32[]{:S(2)}) async-start(), calls=%async_computation.3 | async-start | bytes 8912896 | tf_op jit(solution)/shard_map/all_gather | solution.py:231
  11.1 17.1 %collective-permute-start = (bf16[1024,256]{1,0:T(8,128)(2,1)S(1)}, bf16[1024,256]{1,0:T(8,128)(2,1)S(1)}, u32[]{:S(2)}, u32[]{:S(2)}) collective-permute-start(bf16[1024,256]{1,0:T(8,128)(2,1)S(1)} %bitcast.110), channel_id=1, source_target_pairs={{0,224},{32,0},{64,32},{96,64},{128,96},{160,128},{192,160},{224,1... | collective-permute-start | bytes 1572872 | tf_op jit(solution)/shard_map/ppermute | solution.py:91
  17.6 14.8 %collective-permute-start.2 = (bf16[1024,256]{1,0:T(8,128)(2,1)S(1)}, bf16[1024,256]{1,0:T(8,128)(2,1)S(1)}, u32[]{:S(2)}, u32[]{:S(2)}) collective-permute-start(bf16[1024,256]{1,0:T(8,128)(2,1)S(1)} %bitcast.111), channel_id=1, source_target_pairs={{0,32},{32,64},{64,96},{96,128},{128,160},{160,192},{192,224},{224... | collective-permute-start | bytes 1572872 | tf_op jit(solution)/shard_map/ppermute | solution.py:91
  17.6 17.7 %collective-permute-start.4 = (bf16[1024,256]{1,0:T(8,128)(2,1)S(1)}, bf16[1024,256]{1,0:T(8,128)(2,1)S(1)}, u32[]{:S(2)}, u32[]{:S(2)}) collective-permute-start(bf16[1024,256]{1,0:T(8,128)(2,1)S(1)} %bitcast.112), channel_id=1, source_target_pairs={{0,16},{16,0},{1,17},{17,1},{2,18},{18,2},{3,19},{19,3},{4,20},{20... | collective-permute-start | bytes 1572872 | tf_op jit(solution)/shard_map/ppermute | solution.py:91
  28.1 13.1 %collective-permute-start.1 = (bf16[1024,256]{1,0:T(8,128)(2,1)S(1)}, bf16[1024,256]{1,0:T(8,128)(2,1)}, u32[]{:S(2)}, u32[]{:S(2)}) collective-permute-start(bf16[1024,256]{1,0:T(8,128)(2,1)S(1)} %collective-permute-done.refs_4_), channel_id=1, source_target_pairs={{0,224},{32,0},{64,32},{96,64},{128,96},{160,128},{192,160},{224,1... | collective-permute-start | bytes 1572872 | tf_op jit(solution)/shard_map/ppermute | solution.py:91
  32.4 12.9 %collective-permute-start.3 = (bf16[1024,256]{1,0:T(8,128)(2,1)S(1)}, bf16[1024,256]{1,0:T(8,128)(2,1)}, u32[]{:S(2)}, u32[]{:S(2)}) collective-permute-start(bf16[1024,256]{1,0:T(8,128)(2,1)S(1)} %collective-permute-done.2.refs_2_), channel_id=1, source_target_pairs={{0,32},{32,64},{64,96},{96,128},{128,160},{160,192},{192,224},{224... | collective-permute-start | bytes 1572872 | tf_op jit(solution)/shard_map/ppermute | solution.py:91
  35.2 17.2 %collective-permute-start.5 = (bf16[1024,256]{1,0:T(8,128)(2,1)S(1)}, bf16[1024,256]{1,0:T(8,128)(2,1)}, u32[]{:S(2)}, u32[]{:S(2)}) collective-permute-start(bf16[1024,256]{1,0:T(8,128)(2,1)S(1)} %collective-permute-done.4.refs_10_), channel_id=1, source_target_pairs={{0,224},{32,0},{64,32},{96,64},{128,96},{160,128},{192,160},{224,1... | collective-permute-start | bytes 1572872 | tf_op jit(solution)/shard_map/ppermute | solution.py:91
  36.9 19.7 %collective-permute-start.6 = (bf16[1024,256]{1,0:T(8,128)(2,1)S(1)}, bf16[1024,256]{1,0:T(8,128)(2,1)}, u32[]{:S(2)}, u32[]{:S(2)}) collective-permute-start(bf16[1024,256]{1,0:T(8,128)(2,1)S(1)} %collective-permute-done.4.refs_10_), channel_id=1, source_target_pairs={{0,32},{32,64},{64,96},{96,128},{128,160},{160,192},{192,224},{224... | collective-permute-start | bytes 1572872 | tf_op jit(solution)/shard_map/ppermute | solution.py:91
  41.2 44.0 %collective-permute-start.15 = (bf16[1024,256]{1,0:T(8,128)(2,1)}, bf16[1024,256]{1,0:T(8,128)(2,1)S(1)}, u32[]{:S(2)}, u32[]{:S(2)}) collective-permute-start(bf16[1024,256]{1,0:T(8,128)(2,1)} %collective-permute-done.1.rest_0_.refs_5_), channel_id=1, source_target_pairs={{0,224},{32,0},{64,32},{96,64},{128,96},{160,128},{192,160},{224,1... | collective-permute-start | bytes 1572872 | tf_op jit(solution)/shard_map/ppermute | solution.py:91
  45.3 40.0 %collective-permute-start.16 = (bf16[1024,256]{1,0:T(8,128)(2,1)}, bf16[1024,256]{1,0:T(8,128)(2,1)S(1)}, u32[]{:S(2)}, u32[]{:S(2)}) collective-permute-start(bf16[1024,256]{1,0:T(8,128)(2,1)} %collective-permute-done.3.rest_1_.refs_1_), channel_id=1, source_target_pairs={{0,32},{32,64},{64,96},{96,128},{128,160},{160,192},{192,224},{224... | collective-permute-start | bytes 1572872 | tf_op jit(solution)/shard_map/ppermute | solution.py:91
  52.5 32.8 %collective-permute-start.17 = (bf16[1024,256]{1,0:T(8,128)(2,1)}, bf16[1024,256]{1,0:T(8,128)(2,1)}, u32[]{:S(2)}, u32[]{:S(2)}) collective-permute-start(bf16[1024,256]{1,0:T(8,128)(2,1)} %collective-permute-done.5.rest_2_.refs_11_), channel_id=1, source_target_pairs={{0,224},{32,0},{64,32},{96,64},{128,96},{160,128},{192,160},{224,1... | collective-permute-start | bytes 1572872 | tf_op jit(solution)/shard_map/ppermute | solution.py:91
  56.5 28.8 %collective-permute-start.18 = (bf16[1024,256]{1,0:T(8,128)(2,1)}, bf16[1024,256]{1,0:T(8,128)(2,1)}, u32[]{:S(2)}, u32[]{:S(2)}) collective-permute-start(bf16[1024,256]{1,0:T(8,128)(2,1)} %collective-permute-done.6.rest_3_.refs_9_), channel_id=1, source_target_pairs={{0,32},{32,64},{64,96},{96,128},{128,160},{160,192},{192,224},{224... | collective-permute-start | bytes 1572872 | tf_op jit(solution)/shard_map/ppermute | solution.py:91
  74.5 3.4 %copy-start.3 = (bf16[4096,1024]{1,0:T(8,128)(2,1)S(1)}, bf16[4096,1024]{1,0:T(8,128)(2,1)}, u32[]{:S(2)}) copy-start(bf16[4096,1024]{1,0:T(8,128)(2,1)} %all-gather.2.cloned.1.call-done.panel_hbm) | copy-start | bytes 25165828
  77.9 1.7 copy-start.6
  81.0 4.3 %copy-start.7 = (bf16[1,1,80,128,128]{4,3,2,1,0:T(8,128)(2,1)S(1)}, bf16[1,1,80,128,128]{4,3,2,1,0:T(8,128)(2,1)}, u32[]{:S(2)}) copy-start(bf16[1,1,80,128,128]{4,3,2,1,0:T(8,128)(2,1)} %param.12) | copy-start | bytes 7864324
  81.0 4.3 %copy-start.24 = (s32[1,1,80]{2,1,0:T(1,128)S(1)}, s32[1,1,80]{2,1,0:T(1,128)}, u32[]{:S(2)}) copy-start(s32[1,1,80]{2,1,0:T(1,128)} %param.13) | copy-start | bytes 964
  81.0 4.3 %copy-start.26 = (s32[1,1,80]{2,1,0:T(1,128)S(1)}, s32[1,1,80]{2,1,0:T(1,128)}, u32[]{:S(2)}) copy-start(s32[1,1,80]{2,1,0:T(1,128)} %param.14) | copy-start | bytes 964
  85.2 4.4 %copy-start.1 = (bf16[32,128,512]{2,1,0:T(8,128)(2,1)}, bf16[32,128,512]{2,1,0:T(8,128)(2,1)S(1)}, u32[]{:S(2)}) copy-start(bf16[32,128,512]{2,1,0:T(8,128)(2,1)S(1)} %shard_map.95.rest_4_) | copy-start | bytes 12582916
  85.2 4.4 %copy-start.9 = (bf16[1024,256]{1,0:T(8,128)(2,1)}, bf16[1024,256]{1,0:T(8,128)(2,1)S(1)}, u32[]{:S(2)}) copy-start(bf16[1024,256]{1,0:T(8,128)(2,1)S(1)} %collective-permute-done.15.rest_0_.refs_6_) | copy-start | bytes 1572868
  85.2 4.3 %copy-start.12 = (bf16[1024,256]{1,0:T(8,128)(2,1)}, bf16[1024,256]{1,0:T(8,128)(2,1)S(1)}, u32[]{:S(2)}) copy-start(bf16[1024,256]{1,0:T(8,128)(2,1)S(1)} %collective-permute-done.16.rest_1_.refs_0_) | copy-start | bytes 1572868
  89.6 2.0 copy-start.4
  92.8 13.6 %collective-permute-start.22 = (bf16[512,512]{1,0:T(8,128)(2,1)}, bf16[512,512]{1,0:T(8,128)(2,1)}, u32[]{:S(2)}, u32[]{:S(2)}) collective-permute-start(bf16[512,512]{1,0:T(8,128)(2,1)} %get-tuple-element.19), channel_id=1, source_target_pairs={{0,224},{32,0},{64,32},{96,64},{128,96},{160,128},{192,160},{224,1... | collective-permute-start | bytes 1572872 | tf_op jit(solution)/shard_map/ppermute | solution.py:91
  95.5 17.1 %collective-permute-start.27 = (bf16[1024,256]{1,0:T(8,128)(2,1)}, bf16[1024,256]{1,0:T(8,128)(2,1)S(1)}, u32[]{:S(2)}, u32[]{:S(2)}) collective-permute-start(bf16[1024,256]{1,0:T(8,128)(2,1)} %collective-permute-done.18.rest_3_.refs_8_), channel_id=1, source_target_pairs={{0,32},{32,64},{64,96},{96,128},{128,160},{160,192},{192,224},{224... | collective-permute-start | bytes 1572872 | tf_op jit(solution)/shard_map/ppermute | solution.py:91
  95.5 22.0 %collective-permute-start.28 = (bf16[1024,256]{1,0:T(8,128)(2,1)}, bf16[1024,256]{1,0:T(8,128)(2,1)S(1)}, u32[]{:S(2)}, u32[]{:S(2)}) collective-permute-start(bf16[1024,256]{1,0:T(8,128)(2,1)} %collective-permute-done.17.rest_2_.refs_12_), channel_id=1, source_target_pairs={{0,224},{32,0},{64,32},{96,64},{128,96},{160,128},{192,160},{224,1... | collective-permute-start | bytes 1572872 | tf_op jit(solution)/shard_map/ppermute | solution.py:91
  100.5 17.8 %copy-start.5 = (bf16[32,128,512]{2,1,0:T(8,128)(2,1)S(1)}, bf16[32,128,512]{2,1,0:T(8,128)(2,1)}, u32[]{:S(2)}) copy-start(bf16[32,128,512]{2,1,0:T(8,128)(2,1)} %copy-done.4) | copy-start | bytes 12582916
  100.6 17.8 %copy-start.10 = (bf16[1024,256]{1,0:T(8,128)(2,1)S(1)}, bf16[1024,256]{1,0:T(8,128)(2,1)}, u32[]{:S(2)}) copy-start(bf16[1024,256]{1,0:T(8,128)(2,1)} %copy-done.9) | copy-start | bytes 1572868
  103.1 33.0 %copy-start.15 = (bf16[512,512]{1,0:T(8,128)(2,1)}, bf16[512,512]{1,0:T(8,128)(2,1)S(1)}, u32[]{:S(2)}) copy-start(bf16[512,512]{1,0:T(8,128)(2,1)S(1)} %get-tuple-element.12.below) | copy-start | bytes 1572868
  103.1 32.8 %collective-permute-start.7 = (bf16[512,512]{1,0:T(8,128)(2,1)S(1)}, bf16[512,512]{1,0:T(8,128)(2,1)S(1)}, u32[]{:S(2)}, u32[]{:S(2)}) collective-permute-start(bf16[512,512]{1,0:T(8,128)(2,1)S(1)} %get-tuple-element.10), channel_id=1, source_target_pairs={{0,32},{32,64},{64,96},{96,128},{128,160},{160,192},{192,224},{224... | collective-permute-start | bytes 1572872 | tf_op jit(solution)/shard_map/ppermute | solution.py:91
  107.7 25.6 %copy-start.22 = (bf16[512,512]{1,0:T(8,128)(2,1)}, bf16[512,512]{1,0:T(8,128)(2,1)S(1)}, u32[]{:S(2)}) copy-start(bf16[512,512]{1,0:T(8,128)(2,1)S(1)} %fusion.11.below) | copy-start | bytes 1572868
  118.3 1.0 copy-start.11
  119.4 1.0 copy-start.13
  120.4 1.0 copy-start.18
  121.5 1.0 copy-start.28
  122.5 1.0 copy-start.30
  123.6 1.0 copy-start.32
  124.6 1.0 copy-start.34
  125.6 1.0 copy-start.36
  126.7 9.2 %copy-start.2 = (bf16[32,128,512]{2,1,0:T(8,128)(2,1)S(1)}, bf16[32,128,512]{2,1,0:T(8,128)(2,1)}, u32[]{:S(2)}) copy-start(bf16[32,128,512]{2,1,0:T(8,128)(2,1)} %copy-done.1) | copy-start | bytes 12582916
  126.7 9.4 %copy-start.14 = (bf16[1024,256]{1,0:T(8,128)(2,1)S(1)}, bf16[1024,256]{1,0:T(8,128)(2,1)}, u32[]{:S(2)}) copy-start(bf16[1024,256]{1,0:T(8,128)(2,1)} %copy-done.12) | copy-start | bytes 1572868
  126.7 9.4 %copy-start.19 = (bf16[1,256,1024]{1,2,0:T(8,128)(2,1)S(1)}, bf16[1,256,1024]{1,2,0:T(8,128)(2,1)}, u32[]{:S(2)}) copy-start(bf16[1,256,1024]{1,2,0:T(8,128)(2,1)} %copy-done.17) | copy-start | bytes 1572868
  134.2 15.5 %collective-permute-start.30 = (bf16[512,512]{1,0:T(8,128)(2,1)}, bf16[512,512]{1,0:T(8,128)(2,1)}, u32[]{:S(2)}, u32[]{:S(2)}) collective-permute-start(bf16[512,512]{1,0:T(8,128)(2,1)} %dynamic-slice_bitcast_fusion), channel_id=1, source_target_pairs={{0,1},{1,0},{2,3},{3,2},{4,5},{5,4},{6,7},{7,6},{8,9},{9,8},{10,11... | collective-permute-start | bytes 1572872 | tf_op jit(solution)/shard_map/ppermute | solution.py:91
  136.0 6.8 %copy-start.20 = (bf16[512,512]{1,0:T(8,128)(2,1)}, bf16[512,512]{1,0:T(8,128)(2,1)S(1)}, u32[]{:S(2)}) copy-start(bf16[512,512]{1,0:T(8,128)(2,1)S(1)} %fusion.18.above) | copy-start | bytes 1572868
  144.6 6.3 %collective-permute-start.29 = (bf16[512,512]{1,0:T(8,128)(2,1)}, bf16[512,512]{1,0:T(8,128)(2,1)}, u32[]{:S(2)}, u32[]{:S(2)}) collective-permute-start(bf16[512,512]{1,0:T(8,128)(2,1)} %dynamic-slice_bitcast_fusion.1), channel_id=1, source_target_pairs={{0,1},{1,0},{2,3},{3,2},{4,5},{5,4},{6,7},{7,6},{8,9},{9,8},{10,11... | collective-permute-start | bytes 1572872 | tf_op jit(solution)/shard_map/ppermute | solution.py:91
  144.7 17.7 %collective-permute-start.19 = (bf16[512,512]{1,0:T(8,128)(2,1)}, bf16[512,512]{1,0:T(8,128)(2,1)}, u32[]{:S(2)}, u32[]{:S(2)}) collective-permute-start(bf16[512,512]{1,0:T(8,128)(2,1)} %get-tuple-element.17.above), channel_id=1, source_target_pairs={{0,32},{32,64},{64,96},{96,128},{128,160},{160,192},{192,224},{224... | collective-permute-start | bytes 1572872 | tf_op jit(solution)/shard_map/ppermute | solution.py:91
  144.7 17.7 %collective-permute-start.23 = (bf16[512,512]{1,0:T(8,128)(2,1)}, bf16[512,512]{1,0:T(8,128)(2,1)}, u32[]{:S(2)}, u32[]{:S(2)}) collective-permute-start(bf16[512,512]{1,0:T(8,128)(2,1)} %copy-done.22), channel_id=1, source_target_pairs={{0,224},{32,0},{64,32},{96,64},{128,96},{160,128},{192,160},{224,1... | collective-permute-start | bytes 1572872 | tf_op jit(solution)/shard_map/ppermute | solution.py:91
  150.9 10.0 %copy-start.16 = (bf16[512,512]{1,0:T(8,128)(2,1)S(1)}, bf16[512,512]{1,0:T(8,128)(2,1)}, u32[]{:S(2)}) copy-start(bf16[512,512]{1,0:T(8,128)(2,1)} %copy-done.15) | copy-start | bytes 1572868
  150.9 11.5 %copy-start.21 = (bf16[512,512]{1,0:T(8,128)(2,1)S(1)}, bf16[512,512]{1,0:T(8,128)(2,1)}, u32[]{:S(2)}) copy-start(bf16[512,512]{1,0:T(8,128)(2,1)} %copy-done.20) | copy-start | bytes 1572868
  153.5 24.6 %all-to-all-start = ((bf16[16,32,1024]{2,1,0:T(8,128)(2,1)}), bf16[16,32,1024]{2,1,0:T(8,128)(2,1)}, u32[]{:S(2)}, u32[]{:S(2)}) async-start(bf16[16,32,1024]{2,1,0:T(8,128)(2,1)} %bitcast.120), calls=%async_computation | async-start | bytes 2097152 | tf_op jit(solution)/shard_map/all_to_all | solution.py:211
  160.8 12.5 %collective-permute-start.11 = (bf16[512,512]{1,0:T(8,128)(2,1)S(1)}, bf16[512,512]{1,0:T(8,128)(2,1)}, u32[]{:S(2)}, u32[]{:S(2)}) collective-permute-start(bf16[512,512]{1,0:T(8,128)(2,1)S(1)} %copy-done.16), channel_id=1, source_target_pairs={{0,224},{32,0},{64,32},{96,64},{128,96},{160,128},{192,160},{224,1... | collective-permute-start | bytes 1572872 | tf_op jit(solution)/shard_map/ppermute | solution.py:91
  162.4 13.1 %collective-permute-start.8 = (bf16[512,512]{1,0:T(8,128)(2,1)S(1)}, bf16[512,512]{1,0:T(8,128)(2,1)}, u32[]{:S(2)}, u32[]{:S(2)}) collective-permute-start(bf16[512,512]{1,0:T(8,128)(2,1)S(1)} %copy-done.21), channel_id=1, source_target_pairs={{0,32},{32,64},{64,96},{96,128},{128,160},{160,192},{192,224},{224... | collective-permute-start | bytes 1572872 | tf_op jit(solution)/shard_map/ppermute | solution.py:91
  165.2 21.7 %collective-permute-start.20 = (bf16[512,512]{1,0:T(8,128)(2,1)}, bf16[512,512]{1,0:T(8,128)(2,1)}, u32[]{:S(2)}, u32[]{:S(2)}) collective-permute-start(bf16[512,512]{1,0:T(8,128)(2,1)} %get-tuple-element.15), channel_id=1, source_target_pairs={{0,32},{32,64},{64,96},{96,128},{128,160},{160,192},{192,224},{224... | collective-permute-start | bytes 1572872 | tf_op jit(solution)/shard_map/ppermute | solution.py:91
  165.9 21.0 %collective-permute-start.24 = (bf16[512,512]{1,0:T(8,128)(2,1)}, bf16[512,512]{1,0:T(8,128)(2,1)}, u32[]{:S(2)}, u32[]{:S(2)}) collective-permute-start(bf16[512,512]{1,0:T(8,128)(2,1)} %get-tuple-element.16), channel_id=1, source_target_pairs={{0,224},{32,0},{64,32},{96,64},{128,96},{160,128},{192,160},{224,1... | collective-permute-start | bytes 1572872 | tf_op jit(solution)/shard_map/ppermute | solution.py:91
  180.4 31.5 %all-to-all-start.1 = ((bf16[8,32,1024]{2,1,0:T(8,128)(2,1)}), bf16[8,32,1024]{2,1,0:T(8,128)(2,1)S(1)}, u32[]{:S(2)}, u32[]{:S(2)}) async-start(bf16[8,32,1024]{2,1,0:T(8,128)(2,1)} %broadcast_in_dim.7), calls=%async_computation.1 | async-start | bytes 1048576 | tf_op jit(solution)/shard_map/all_to_all | solution.py:214
  184.1 24.9 %collective-permute-start.9 = (bf16[512,512]{1,0:T(8,128)(2,1)}, bf16[512,512]{1,0:T(8,128)(2,1)}, u32[]{:S(2)}, u32[]{:S(2)}) collective-permute-start(bf16[512,512]{1,0:T(8,128)(2,1)} %get-tuple-element.8), channel_id=1, source_target_pairs={{0,32},{32,64},{64,96},{96,128},{128,160},{160,192},{192,224},{224... | collective-permute-start | bytes 1572872 | tf_op jit(solution)/shard_map/ppermute | solution.py:91
  185.4 23.7 %collective-permute-start.12 = (bf16[512,512]{1,0:T(8,128)(2,1)S(1)}, bf16[512,512]{1,0:T(8,128)(2,1)}, u32[]{:S(2)}, u32[]{:S(2)}) collective-permute-start(bf16[512,512]{1,0:T(8,128)(2,1)S(1)} %get-tuple-element.9), channel_id=1, source_target_pairs={{0,224},{32,0},{64,32},{96,64},{128,96},{160,128},{192,160},{224,1... | collective-permute-start | bytes 1572872 | tf_op jit(solution)/shard_map/ppermute | solution.py:91
  213.1 21.5 %all-to-all-start.2 = ((bf16[16,32,1024]{2,1,0:T(8,128)(2,1)}), bf16[16,32,1024]{2,1,0:T(8,128)(2,1)S(1)}, u32[]{:S(2)}, u32[]{:S(2)}) async-start(bf16[16,32,1024]{2,1,0:T(8,128)(2,1)} %broadcast_in_dim.8), calls=%async_computation.2 | async-start | bytes 2097152 | tf_op jit(solution)/shard_map/all_to_all | solution.py:217
  219.8 18.7 %collective-permute-start.25 = (bf16[512,512]{1,0:T(8,128)(2,1)}, bf16[512,512]{1,0:T(8,128)(2,1)}, u32[]{:S(2)}, u32[]{:S(2)}) collective-permute-start(bf16[512,512]{1,0:T(8,128)(2,1)} %get-tuple-element.14), channel_id=1, source_target_pairs={{0,224},{32,0},{64,32},{96,64},{128,96},{160,128},{192,160},{224,1... | collective-permute-start | bytes 1572872 | tf_op jit(solution)/shard_map/ppermute | solution.py:91
  219.9 18.6 %collective-permute-start.21 = (bf16[512,512]{1,0:T(8,128)(2,1)}, bf16[512,512]{1,0:T(8,128)(2,1)}, u32[]{:S(2)}, u32[]{:S(2)}) collective-permute-start(bf16[512,512]{1,0:T(8,128)(2,1)} %get-tuple-element.13), channel_id=1, source_target_pairs={{0,32},{32,64},{64,96},{96,128},{128,160},{160,192},{192,224},{224... | collective-permute-start | bytes 1572872 | tf_op jit(solution)/shard_map/ppermute | solution.py:91
  221.4 20.7 %collective-permute-start.13 = (bf16[512,512]{1,0:T(8,128)(2,1)}, bf16[512,512]{1,0:T(8,128)(2,1)}, u32[]{:S(2)}, u32[]{:S(2)}) collective-permute-start(bf16[512,512]{1,0:T(8,128)(2,1)} %get-tuple-element.7), channel_id=1, source_target_pairs={{0,224},{32,0},{64,32},{96,64},{128,96},{160,128},{192,160},{224,1... | collective-permute-start | bytes 1572872 | tf_op jit(solution)/shard_map/ppermute | solution.py:91
  222.7 20.4 %collective-permute-start.10 = (bf16[512,512]{1,0:T(8,128)(2,1)}, bf16[512,512]{1,0:T(8,128)(2,1)}, u32[]{:S(2)}, u32[]{:S(2)}) collective-permute-start(bf16[512,512]{1,0:T(8,128)(2,1)} %get-tuple-element.6), channel_id=1, source_target_pairs={{0,32},{32,64},{64,96},{96,128},{128,160},{160,192},{192,224},{224... | collective-permute-start | bytes 1572872 | tf_op jit(solution)/shard_map/ppermute | solution.py:91
  234.6 21.4 %collective-permute-start.31 = (bf16[512,1024]{1,0:T(8,128)(2,1)S(1)}, bf16[512,1024]{1,0:T(8,128)(2,1)}, u32[]{:S(2)}, u32[]{:S(2)}) collective-permute-start(bf16[512,1024]{1,0:T(8,128)(2,1)S(1)} %bitcast.119), channel_id=1, source_target_pairs={{0,1},{1,0},{2,3},{3,2},{4,5},{5,4},{6,7},{7,6},{8,9},{9,8},{10,11... | collective-permute-start | bytes 3145736 | tf_op jit(solution)/shard_map/ppermute | solution.py:91
  240.4 8.5 %collective-permute-start.26 = (bf16[256,512]{1,0:T(8,128)(2,1)}, bf16[256,512]{1,0:T(8,128)(2,1)S(1)}, u32[]{:S(2)}, u32[]{:S(2)}) collective-permute-start(bf16[256,512]{1,0:T(8,128)(2,1)} %fusion.25), channel_id=1, source_target_pairs={{0,16},{16,0},{1,17},{17,1},{2,18},{18,2},{3,19},{19,3},{4,20},{20... | collective-permute-start | bytes 786440 | tf_op jit(solution)/shard_map/ppermute | solution.py:91
  245.0 8.1 %collective-permute-start.14 = (bf16[256,512]{1,0:T(8,128)(2,1)}, bf16[256,512]{1,0:T(8,128)(2,1)}, u32[]{:S(2)}, u32[]{:S(2)}) collective-permute-start(bf16[256,512]{1,0:T(8,128)(2,1)} %fusion.24), channel_id=1, source_target_pairs={{0,16},{16,0},{1,17},{17,1},{2,18},{18,2},{3,19},{19,3},{4,20},{20... | collective-permute-start | bytes 786440 | tf_op jit(solution)/shard_map/ppermute | solution.py:91
  (9 other events, 7.1 us)
Sparse Core Ops, SparseCore 0:
  10.4 64.0 all-gather.1

commit v3 on v0

v3 whole, which is shorter than its diff:
```python
import functools

import jax
import jax.numpy as jnp
from jax import lax
from jax.experimental import pallas as pl
from jax.experimental.pallas import tpu as pltpu
from jax.sharding import Mesh, PartitionSpec as P

ROW = ("z", "yh")
COL = ("x", "yl", "core")
SIDE = ("yh", "x", "yl")
GROUP = 8
STEP = 256
CHUNKS = 2
REACH = 3


def silu_grad(grad_out, preact):
    pre_value = preact.astype(jnp.float32)
    sigmoid_val = jax.nn.sigmoid(pre_value)
    scaled = grad_out.astype(jnp.float32) * sigmoid_val * (1.0 + pre_value * (1.0 - sigmoid_val))
    return scaled.astype(jnp.bfloat16)


def tile_kernel(chunks, count_ref, send_ref, row_ref, col_ref, blocks_hbm, panel_hbm, *refs):
    outs, (total, blocks_ref, panel_ref, stage, sems) = refs[:-5], refs[-5:]
    _, tiles, size, width = stage.shape
    count = count_ref[0]
    loads = [pltpu.make_async_copy(blocks_hbm, blocks_ref, sems.at[0])]
    for c in range(chunks):
        loads.append(pltpu.make_async_copy(
            panel_hbm.at[:, c * width:(c + 1) * width], panel_ref.at[c], sems.at[1 + c]
        ))
    for copy in loads:
        copy.start()
    total[...] = jnp.zeros_like(total)
    loads[0].wait()
    leaving = []
    for c in range(chunks):
        loads[1 + c].wait()

        def add_group(step, carry):
            products = []
            for u in range(GROUP):
                slot = step * GROUP + u
                start = pl.multiple_of(row_ref[slot] * size, size)
                products.append(lax.dot_general(
                    blocks_ref[slot], panel_ref[c, pl.ds(start, size), :], (((0,), (0,)), ((), ())),
                    preferred_element_type=jnp.float32,
                ))
            for u in range(GROUP):
                slot = step * GROUP + u
                place = jnp.where(slot < count, col_ref[slot], tiles)
                total[place] += products[u]
            return carry

        lax.fori_loop(0, (count + GROUP - 1) // GROUP, add_group, 0)

        def store(tile, carry):
            stage[c, tile] = total[tile].astype(stage.dtype)
            total[tile] = jnp.zeros((size, width), jnp.float32)
            return carry

        lax.fori_loop(0, tiles, store, 0)
        whole, *pieces = outs[3 * c:3 * c + 3]
        first = 1 + chunks + 3 * c
        for i, ref in enumerate(pieces):
            start = send_ref[2 * c + i] * ref.shape[0]
            leaving.append(pltpu.make_async_copy(stage.at[c, pl.ds(start, ref.shape[0])], ref, sems.at[first + i]))
        leaving.append(pltpu.make_async_copy(stage.at[c], whole, sems.at[first + 2]))
        for copy in leaving[-3:]:
            copy.start()
    for copy in leaving:
        copy.wait()


def tile_sum(panel, chunks, blocks, row_ids, col_ids, used_count, col_tiles, send):
    slots, size, _ = blocks.shape
    depth = panel.shape[0]
    width = panel.shape[1] // chunks
    piece = col_tiles // lax.axis_size("z")
    hbm = pl.BlockSpec(memory_space=pl.ANY)
    outs = pl.pallas_call(
        functools.partial(tile_kernel, chunks),
        out_shape=[jax.ShapeDtypeStruct((n, size, width), jnp.bfloat16) for n in (col_tiles, piece, piece)] * chunks,
        in_specs=[pl.BlockSpec(memory_space=pltpu.SMEM)] * 4 + [hbm] * 2,
        out_specs=[hbm] * (3 * chunks),
        scratch_shapes=[
            pltpu.VMEM((col_tiles + 1, size, width), jnp.float32),
            pltpu.VMEM(blocks.shape, jnp.bfloat16),
            pltpu.VMEM((chunks, depth, width), jnp.bfloat16),
            pltpu.VMEM((chunks, col_tiles, size, width), jnp.bfloat16),
            pltpu.SemaphoreType.DMA((1 + 4 * chunks,)),
        ],
        compiler_params=pltpu.CompilerParams(vmem_limit_bytes=56 * 2**20),
        cost_estimate=pl.CostEstimate(flops=1, bytes_accessed=1, transcendentals=0),
    )(used_count, send, row_ids, col_ids, blocks, panel)
    return [outs[3 * c:3 * c + 3] for c in range(chunks)]


def behind(value, others):
    return lax.optimization_barrier((value, others))[0]


def shift(value, axis, way):
    size = lax.axis_size(axis)
    return lax.ppermute(value, axis, [(i, (i + way) % size) for i in range(size)])


def row_sum(partial, pieces, ways):
    size = lax.axis_size("z")
    here = lax.axis_index("z")

    def own(place):
        return lax.dynamic_index_in_dim(partial, jnp.bitwise_and(place, size - 1), 0, keepdims=False)

    arrived = []
    sent = [[] for _ in range(size // 2)]
    for moving, (way, hops) in zip(pieces, ways):
        for hop in range(hops):
            sent[hop].append(moving)
            moving = shift(moving, "z", way)
            left = hops - 1 - hop
            if left:
                moving = (moving.astype(jnp.float32) + own(here + way * left).astype(jnp.float32)).astype(jnp.bfloat16)
        arrived.append(moving)
    arrived.append(own(here))
    half = lax.axis_index("yh")

    def total(which):
        halves = [lax.dynamic_index_in_dim(t.reshape(2, -1, t.shape[-1]), which, 0, keepdims=False) for t in arrived]
        return sum(t.astype(jnp.float32) for t in halves)

    other = shift(total(1 - half).astype(jnp.bfloat16), "yh", 1)
    mixed = (total(half) + other.astype(jnp.float32)).astype(jnp.bfloat16)
    return mixed, sent


def gather_features(turned, reach):
    found = []
    for start in (turned, shift(turned, "yh", 1)):
        if found:
            start = behind(start, [found[0][1], found[0][-1]])
        near = {0: start}
        for k in range(1, reach + 1):
            near[k] = shift(near[k - 1], "z", -1)
            near[-k] = shift(near[1 - k], "z", 1)
        found.append(near)
    return found


def term_kernel(chunks, reach, place_ref, *refs):
    partials, refs = refs[:chunks], refs[chunks:]
    passing, refs = refs[:2 * chunks], refs[2 * chunks:]
    features, (out_ref, total, left, nodes, sems) = refs[:-5], refs[-5:]
    z, yh, first = place_ref[0], place_ref[1], place_ref[2]
    rows = out_ref.shape[0]
    count = 2 * reach + 1
    depth = features[0].shape[1]
    width = nodes.shape[2]
    groups = []
    used = 0
    for i in range(count):
        group = []
        for h in range(2):
            b = 2 * i + h
            at = slice(b * depth, (b + 1) * depth)
            source = features[h * count + i].at[pl.ds(pl.multiple_of(first * rows, rows), rows), :]
            group.append(pltpu.make_async_copy(source, left.at[:, at], sems.at[used]))
            used += 1
            half = pl.ds(pl.multiple_of(jnp.bitwise_xor(yh, h) * depth, depth), depth)
            for c in range(chunks):
                if abs(i - reach) == reach:
                    source = passing[2 * c + (i > reach)].at[half, :]
                else:
                    source = partials[c].at[jnp.bitwise_and(z + (i - reach), partials[c].shape[0] - 1), half, :]
                group.append(pltpu.make_async_copy(source, nodes.at[c, at, :], sems.at[used]))
                used += 1
        groups.append(group)
    for group in groups:
        for copy in group:
            copy.start()
    steps = [(0, 1), (1, 3), (3, 5), (5, count)]
    for step, (low, high) in enumerate(steps):
        for group in groups[low:high]:
            for copy in group:
                copy.wait()
        inner = slice(low * 2 * depth, high * 2 * depth)

        def block(index, carry):
            at = pl.ds(pl.multiple_of(index * STEP, STEP), STEP)
            for c in range(chunks):
                columns = slice(c * width, (c + 1) * width)
                product = jnp.dot(left[at, inner], nodes[c, inner, :], preferred_element_type=jnp.float32)
                if step:
                    product = total[at, columns] + product
                if step < len(steps) - 1:
                    total[at, columns] = product
                else:
                    out_ref[at, columns] = product.astype(out_ref.dtype)
            return carry

        lax.fori_loop(0, rows // STEP, block, 0)


def weight_terms(features, partials, passing, reach, place):
    distances = list(range(-reach, reach + 1))
    features = [near[k] for near in features for k in distances]
    height, depth = features[0].shape
    width = partials[0].shape[2]
    chunks = len(partials)
    blocks = len(features)
    operands = list(partials) + [p for pair in passing for p in pair] + features
    return pl.pallas_call(
        functools.partial(term_kernel, chunks, reach),
        out_shape=jax.ShapeDtypeStruct((height // 2, chunks * width), jnp.bfloat16),
        in_specs=[pl.BlockSpec(memory_space=pltpu.SMEM)] + [pl.BlockSpec(memory_space=pl.ANY)] * len(operands),
        out_specs=pl.BlockSpec(memory_space=pltpu.VMEM),
        scratch_shapes=[
            pltpu.VMEM((height // 2, chunks * width), jnp.float32),
            pltpu.VMEM((height // 2, blocks * depth), jnp.bfloat16),
            pltpu.VMEM((chunks, blocks * depth, width), jnp.bfloat16),
            pltpu.SemaphoreType.DMA(((1 + chunks) * blocks,)),
        ],
        compiler_params=pltpu.CompilerParams(vmem_limit_bytes=56 * 2**20),
        cost_estimate=pl.CostEstimate(flops=1, bytes_accessed=1, transcendentals=0),
    )(place, *operands)


def assemble_kernel(core_ref, mine_ref, other_ref, out_ref):
    mine = core_ref[0] == pl.program_id(0)
    out_ref[...] = jnp.where(mine, mine_ref[...], other_ref[...]).astype(out_ref.dtype)


def assemble(mine, other):
    rows, width = mine.shape
    steps = 2
    half = pl.BlockSpec((rows // steps, width), lambda h, i: (i, 0))
    return pl.pallas_call(
        assemble_kernel,
        grid=(2, steps),
        out_shape=jax.ShapeDtypeStruct((2 * rows, width), jnp.float32),
        in_specs=[pl.BlockSpec(memory_space=pltpu.SMEM), half, half],
        out_specs=pl.BlockSpec((rows // steps, width), lambda h, i: (h * steps + i, 0)),
    )(lax.axis_index("core").reshape(1), mine, other)


def sum_everywhere(mine, other, second, third):
    side = lax.axis_size(SIDE)
    depth = lax.axis_size("z")
    part = mine.astype(jnp.float32) + shift(other, "core", 1).astype(jnp.float32)
    part = part.astype(jnp.bfloat16).reshape(side, -1, part.shape[-1])
    part = lax.all_to_all(part, SIDE, 0, 0, tiled=True)
    part = jnp.sum(part.astype(jnp.float32), axis=0).astype(jnp.bfloat16)
    part = behind(part, second)
    part = lax.all_to_all(jnp.broadcast_to(part[None], (depth,) + part.shape), "z", 0, 0, tiled=True)
    part = jnp.sum(part.astype(jnp.float32), axis=0).astype(jnp.bfloat16)
    part = behind(part, third)
    half = lax.all_to_all(jnp.broadcast_to(part[None], (side,) + part.shape), SIDE, 0, 0, tiled=True)
    half = half.reshape(-1, half.shape[-1])
    return assemble(half, shift(half, "core", 1))


def per_device(grad_out, preact, features, weight, tile_values, tile_row, tile_col, tile_count):
    size = tile_values.shape[-1]
    width = grad_out.shape[-1] // CHUNKS
    col_tiles = features.shape[1] * lax.axis_size(ROW) // size
    tiles = (tile_values[0, 0], tile_row[0, 0], tile_col[0, 0], tile_count[0], col_tiles)
    z, depth = lax.axis_index("z"), lax.axis_size("z")

    panel = lax.all_gather(silu_grad(grad_out[0], preact[0]), COL, axis=0, tiled=True)
    near = gather_features(features[0].T, REACH)
    ways = (((1, 4), (-1, 3)), ((1, 3), (-1, 4)))
    send = jnp.stack([jnp.bitwise_and(z + way * hops, depth - 1) for pair in ways for way, hops in pair])
    send = behind(send, [near[1][2], near[1][-2]])
    partials = []
    passing = []
    mixed = []
    sent = [[] for _ in range(depth // 2)]
    for (whole, *pieces), pair in zip(tile_sum(panel, CHUNKS, *tiles, send), ways):
        partials.append(whole.reshape(depth, -1, width))
        total, moves = row_sum(partials[-1], [p.reshape(-1, width) for p in pieces], pair)
        mixed.append(total)
        for hop, sums in enumerate(moves):
            sent[hop] += sums
        far = {way: moves[hops - REACH][i] for i, (way, hops) in enumerate(pair)}
        passing.append((far[-1], far[1]))
    core = lax.axis_index("core")
    theirs, ours = [jnp.stack([z, lax.axis_index("yh"), half]) for half in (1 - core, core)]
    theirs = weight_terms(near, partials, passing, REACH, theirs)
    ours = weight_terms(near, partials, passing, REACH, behind(ours, [theirs] + sent[1]))
    grad_weight = sum_everywhere(ours, theirs, sent[2], sent[3])
    grad_in = lax.dot_general(
        jnp.concatenate(mixed, axis=1), weight, (((1,), (1,)), ((), ())), preferred_element_type=jnp.float32
    )
    return (grad_in.astype(jnp.bfloat16)[None], grad_weight)


def solution(mesh):
    devices = mesh.devices.reshape(8, 2, 4, 2, 2)
    fine = Mesh(devices, ROW + COL)
    return jax.shard_map(
        per_device,
        mesh=fine,
        in_specs=(
            P(ROW, COL, None),
            P(ROW, COL, None),
            P(COL, ROW, None),
            P(),
            P(ROW, COL, None, None, None),
            P(ROW, COL, None),
            P(ROW, COL, None),
            P(ROW, COL),
        ),
        out_specs=(P(COL, ROW, None), P()),
        check_vma=False,
    )
```

time: 752 us -> 268 us (0.36)
  waiting for transfers between devices: 543 us -> 99.2 us
  other arithmetic: 103 us -> 28.1 us
  starting transfers between devices: 0.12 us -> 57.3 us
  local copies, waits for them, and re-layouts: 50.1 us -> 6.19 us
  Pallas kernels: 0 us -> 39.2 us
  matrix products: 39.4 us -> 1.59 us
  blocking collectives: 0 us -> 17.4 us
    psum x1 -> x0, waiting for transfers between devices: 269 us -> none  [per_device(): grad_weight = lax.psum(local_weight, ('row', 'col'))]
    reduce_scatter x1 -> x0, waiting for transfers between devices: 220 us -> none  [per_device(): lax.psum_scatter(partial_sum.astype(jnp.bfloat16), 'row', scatter_dimensi...]
    scatter-add x5 -> x0, other arithmetic: 91 us -> none  [add_group(): return total.at[group_cols].add(product)]
    ppermute x0 -> x31, waiting for transfers between devices: none -> 77.8 us  [shift(): lax.ppermute(value, axis, [(i, (i + way) % size) for i in range(size)])]
    ppermute x0 -> x31, starting transfers between devices: none -> 46.4 us  [shift(): lax.ppermute(value, axis, [(i, (i + way) % size) for i in range(size)])]
    pallas_call x0 -> x4, Pallas kernels: none -> 39.2 us  [the longest x2 17.3 us: weight_terms(): pl.pallas_call(functools.partial(term_kernel, chunks, reach), out_shape=j...]
    all_gather x1, waiting for transfers between devices: 54.4 us -> 16.3 us  [per_device(): lax.all_gather(silu_grad(grad_out[0], preact[0]), COL, axis=0, tiled=True)]
    dot_general x7 -> x1, matrix products: 39.4 us -> 1.59 us  [per_device(): lax.dot_general(jnp.concatenate(mixed, axis=1), weight, (((1,), (1,)), ((...]
  transfers between devices with their start and end apart: 3 -> 34, of which waited for: 3 -> 17; matrix products, arithmetic and copies ran while one was open for 1% -> 12% of each run, Pallas kernels for 0% -> 13%
where the time goes in v3:
time: 268 us; the launch traced here: 264 us
  waiting for transfers between devices  99.2 us (37%)
  starting transfers between devices  57.3 us (21%)
  Pallas kernels  39.2 us (15%)
  other arithmetic  28.1 us (10%)
  blocking collectives  17.4 us (6%)
  between operations  14.9 us (6%)
  local copies, waits for them, and re-layouts  6.19 us (2%)
    ppermute x31, waiting for transfers between devices, shift(): lax.ppermute(value, axis, [(i, (i + way) % size) for i in range(size)])  77.8 us
    ppermute x31, starting transfers between devices, shift(): lax.ppermute(value, axis, [(i, (i + way) % size) for i in range(size)])  46.4 us
    all_to_all x1, blocking collectives, sum_everywhere(): lax.all_to_all(jnp.broadcast_to(part[None], (depth,) + part.shape), 'z',...  17.4 us
    pallas_call x2, Pallas kernels, weight_terms(): pl.pallas_call(functools.partial(term_kernel, chunks, reach), out_shape=j...  17.3 us
    pallas_call x1, Pallas kernels, tile_sum(): pl.pallas_call(functools.partial(tile_kernel, chunks), out_shape=[jax.Sha...  17.2 us
    all_gather x1, waiting for transfers between devices, per_device(): lax.all_gather(silu_grad(grad_out[0], preact[0]), COL, axis=0, tiled=True)  16.3 us
    convert_element_type x6, other arithmetic, row_sum(): (moving.astype(jnp.float32) + own(here + way * left).astype(jnp.float32))...  14.7 us
    all_to_all x1, starting transfers between devices, sum_everywhere(): lax.all_to_all(jnp.broadcast_to(part[None], (side,) + part.shape), SIDE,...  5.87 us
  transfers between devices with their start and end apart: 34, of which 17 were waited for; matrix products, arithmetic and copies ran while one was open for 12% of the time, Pallas kernels for 13%

profile of v3, /device:TPU:1, one launch (start us, length us, event | category | flops | bytes accessed | tf_op | source)
XLA Modules:
  0.0 264.0 jit_solution(12957664455995141623)
XLA Ops:
  7.2 2.6 fusion.6
  9.8 1.2 copy.11
  11.1 6.5 %collective-permute-start.1 = (bf16[1024,256]{1,0:T(8,128)(2,1)S(1)}, bf16[1024,256]{1,0:T(8,128)(2,1)S(1)}, u32[]{:S(2)}, u32[]{:S(2)}) collective-permute-start(bf16[1024,256]{1,0:T(8,128)(2,1)S(1)} %bitcast.93), channel_id=1, source_target_pairs={{0,224},{32,0},{64,32},{96,64},{128,96},{160,128},{192,160},{224,1... | collective-permute-start | bytes 1572872 | tf_op jit(solution)/shard_map/ppermute | solution.py:108
  17.6 2.9 %collective-permute-start = (bf16[1024,256]{1,0:T(8,128)(2,1)S(1)}, bf16[1024,256]{1,0:T(8,128)(2,1)S(1)}, u32[]{:S(2)}, u32[]{:S(2)}) collective-permute-start(bf16[1024,256]{1,0:T(8,128)(2,1)S(1)} %bitcast.95), channel_id=1, source_target_pairs={{0,16},{16,0},{1,17},{17,1},{2,18},{18,2},{3,19},{19,3},{4,20},{20... | collective-permute-start | bytes 1572872 | tf_op jit(solution)/shard_map/ppermute | solution.py:108
  20.5 7.7 %collective-permute-done.1.refs_10_ = bf16[1024,256]{1,0:T(8,128)(2,1)S(1)} collective-permute-done((bf16[1024,256]{1,0:T(8,128)(2,1)S(1)}, bf16[1024,256]{1,0:T(8,128)(2,1)S(1)}, u32[]{:S(2)}, u32[]{:S(2)}) %collective-permute-start.1) | collective-permute-done | bytes 524320 | tf_op jit(solution)/shard_map/ppermute | solution.py:108
  28.2 3.2 %collective-permute-done.2.refs_8_ = bf16[1024,256]{1,0:T(8,128)(2,1)} collective-permute-done((bf16[1024,256]{1,0:T(8,128)(2,1)S(1)}, bf16[1024,256]{1,0:T(8,128)(2,1)}, u32[]{:S(2)}, u32[]{:S(2)}) %collective-permute-start.2) | collective-permute-done | bytes 524320 | tf_op jit(solution)/shard_map/ppermute | solution.py:108
  31.4 3.9 %collective-permute-done.refs_16_ = bf16[1024,256]{1,0:T(8,128)(2,1)S(1)} collective-permute-done((bf16[1024,256]{1,0:T(8,128)(2,1)S(1)}, bf16[1024,256]{1,0:T(8,128)(2,1)S(1)}, u32[]{:S(2)}, u32[]{:S(2)}) %collective-permute-start) | collective-permute-done | bytes 524320 | tf_op jit(solution)/shard_map/ppermute | solution.py:108
  35.2 1.6 collective-permute-start.3
  36.9 7.1 %collective-permute-done.3.refs_17_ = bf16[1024,256]{1,0:T(8,128)(2,1)} collective-permute-done((bf16[1024,256]{1,0:T(8,128)(2,1)S(1)}, bf16[1024,256]{1,0:T(8,128)(2,1)}, u32[]{:S(2)}, u32[]{:S(2)}) %collective-permute-start.3) | collective-permute-done | bytes 524320 | tf_op jit(solution)/shard_map/ppermute | solution.py:108
  44.0 2.3 collective-permute-start.4
  46.9 0.7 pad_add_fusion.send_ref
  47.5 2.7 %collective-permute-start.25 = (bf16[1024,256]{1,0:T(8,128)(2,1)S(1)}, bf16[1024,256]{1,0:T(8,128)(2,1)}, u32[]{:S(2)}, u32[]{:S(2)}) collective-permute-start(bf16[1024,256]{1,0:T(8,128)(2,1)S(1)} %collective-permute-done.1.refs_10_), channel_id=1, source_target_pairs={{0,224},{32,0},{64,32},{96,64},{128,96},{160,128},{192,160},{224,1... | collective-permute-start | bytes 1572872 | tf_op jit(solution)/shard_map/ppermute | solution.py:108
  50.2 4.7 %collective-permute-done.4.refs_18_ = bf16[1024,256]{1,0:T(8,128)(2,1)} collective-permute-done((bf16[1024,256]{1,0:T(8,128)(2,1)}, bf16[1024,256]{1,0:T(8,128)(2,1)}, u32[]{:S(2)}, u32[]{:S(2)}) %collective-permute-start.4) | collective-permute-done | bytes 524320 | tf_op jit(solution)/shard_map/ppermute | solution.py:108
  54.9 3.4 %collective-permute-done.6.refs_14_ = bf16[1024,256]{1,0:T(8,128)(2,1)} collective-permute-done((bf16[1024,256]{1,0:T(8,128)(2,1)}, bf16[1024,256]{1,0:T(8,128)(2,1)}, u32[]{:S(2)}, u32[]{:S(2)}) %collective-permute-start.6) | collective-permute-done | bytes 524320 | tf_op jit(solution)/shard_map/ppermute | solution.py:108
  58.3 16.3 %all-gather.2.cloned.1.call-done.panel_hbm = bf16[4096,1024]{1,0:T(8,128)(2,1)} async-done(((bf16[256,1024]{1,0:T(8,128)(2,1)}), bf16[4096,1024]{1,0:T(8,128)(2,1)}) %all-gather.2.cloned.1.call-update) | async-done | bytes 8388624 | tf_op jit(solution)/shard_map/all_gather | solution.py:272
  74.5 17.2 %shard_map.95 = (bf16[32,128,512]{2,1,0:T(8,128)(2,1)}, bf16[4,128,512]{2,1,0:T(8,128)(2,1)}, bf16[4,128,512]{2,1,0:T(8,128)(2,1)}, bf16[32,128,512]{2,1,0:T(8,1...) custom-call(s32[1]{0:T(128)} %bitcast.80.count_ref, s32[4]{0:T(128)} %pad_add_fusion.send_ref, ...), custom_call_target="tpu_custom_call" | custom-call | flops 1 | bytes 1 | tf_op jit(solution)/shard_map/pallas_call | solution.py:84
  91.9 2.7 %collective-permute-start.18 = (bf16[512,512]{1,0:T(8,128)(2,1)}, bf16[512,512]{1,0:T(8,128)(2,1)}, u32[]{:S(2)}, u32[]{:S(2)}) collective-permute-start(bf16[512,512]{1,0:T(8,128)(2,1)} %bitcast.110), channel_id=1, source_target_pairs={{0,224},{32,0},{64,32},{96,64},{128,96},{160,128},{192,160},{224,1... | collective-permute-start | bytes 1572872 | tf_op jit(solution)/shard_map/ppermute | solution.py:108
  94.6 1.4 collective-permute-start.26
  96.1 11.2 %collective-permute-done.7 = bf16[512,512]{1,0:T(8,128)(2,1)} collective-permute-done((bf16[512,512]{1,0:T(8,128)(2,1)}, bf16[512,512]{1,0:T(8,128)(2,1)}, u32[]{:S(2)}, u32[]{:S(2)}) %collective-permute-start.7) | collective-permute-done | bytes 524320 | tf_op jit(solution)/shard_map/ppermute | solution.py:108
  107.3 0.7 pad_add_fusion.1
  107.9 1.3 fusion.16.refs_3_
  109.3 9.3 %collective-permute-done.24.refs_6_ = bf16[1024,256]{1,0:T(8,128)(2,1)S(1)} collective-permute-done((bf16[1024,256]{1,0:T(8,128)(2,1)}, bf16[1024,256]{1,0:T(8,128)(2,1)S(1)}, u32[]{:S(2)}, u32[]{:S(2)}) %collective-permute-start.24) | collective-permute-done | bytes 524320 | tf_op jit(solution)/shard_map/ppermute | solution.py:108
  118.6 1.5 collective-permute-start.8
  120.1 2.1 fusion.9.refs_4_
  122.2 6.3 %collective-permute-done.27.refs_13_ = bf16[1024,256]{1,0:T(8,128)(2,1)} collective-permute-done((bf16[1024,256]{1,0:T(8,128)(2,1)}, bf16[1024,256]{1,0:T(8,128)(2,1)}, u32[]{:S(2)}, u32[]{:S(2)}) %collective-permute-start.27) | collective-permute-done | bytes 524320 | tf_op jit(solution)/shard_map/ppermute | solution.py:108
  128.5 0.7 collective-permute-done.28.refs_19_
  129.2 8.7 %shard_map.96 = bf16[512,1024]{1,0:T(8,128)(2,1)} custom-call(s32[3]{0:T(128)} %get-tuple-element.33.place_ref, bf16[8,512,512]{2,1,0:T(8,128)(2,1)} %bitcast.88, bf16[8,512,512]{2,1,0:T(8,128)(2,1)} %bitcast.82, bf16[512,512]{1,0:T(8,128)(2,1)} %bitcast.102, bf16[512,512]{1,0:T(8,128)(2,1)} %copy-done.2, bf16[512,512]{1,0:T(8,128)(2,1)} %fusion.9.refs_4_, ...), custom_call_target="tpu_custom_call" | custom-call | flops 1 | bytes 1 | tf_op jit(solution)/shard_map/pallas_call | solution.py:215
  138.0 0.5 collective-permute-start.29
  138.5 3.2 %collective-permute-start.19 = (bf16[512,512]{1,0:T(8,128)(2,1)S(1)}, bf16[512,512]{1,0:T(8,128)(2,1)}, u32[]{:S(2)}, u32[]{:S(2)}) collective-permute-start(bf16[512,512]{1,0:T(8,128)(2,1)S(1)} %copy-done.3), channel_id=1, source_target_pairs={{0,224},{32,0},{64,32},{96,64},{128,96},{160,128},{192,160},{224,1... | collective-permute-start | bytes 1572872 | tf_op jit(solution)/shard_map/ppermute | solution.py:108
  141.7 2.8 %fusion.15 = (bf16[512,512]{1,0:T(8,128)(2,1)}, bf16[512,512]{1,0:T(8,128)(2,1)}) fusion(bf16[512,512]{1,0:T(8,128)(2,1)} %collective-permute-done.8, bf16[8,512,512]{2,1,0:T(8,128)(2,1)} %bitcast.89, s32[]{:T(128)S(6)} %select_n.45, s32[]{:T(128)S(6)} %select_n.48, bf16[512,512]{1,0:T(8,128)(2,1)} %collective-permute-done.11), kind=kLoop, calls=%fused_computation.28 | loop fusion | flops 2097152 | bytes 3145736 | tf_op jit(solution)/shard_map/convert_element_type | solution.py:126
  144.5 1.4 collective-permute-start.12
  145.9 8.0 %collective-permute-done.15 = bf16[512,512]{1,0:T(8,128)(2,1)} collective-permute-done((bf16[512,512]{1,0:T(8,128)(2,1)}, bf16[512,512]{1,0:T(8,128)(2,1)}, u32[]{:S(2)}, u32[]{:S(2)}) %collective-permute-start.15) | collective-permute-done | bytes 524320 | tf_op jit(solution)/shard_map/ppermute | solution.py:108
  153.8 0.1 collective-permute-done.19
  153.9 2.8 %fusion.11 = (bf16[512,512]{1,0:T(8,128)(2,1)}, bf16[512,512]{1,0:T(8,128)(2,1)}) fusion(bf16[512,512]{1,0:T(8,128)(2,1)} %collective-permute-done.15, bf16[8,512,512]{2,1,0:T(8,128)(2,1)} %bitcast.83, s32[]{:T(128)S(6)} %select_n.45, s32[]{:T(128)S(6)} %select_n.48, bf16[512,512]{1,0:T(8,128)(2,1)} %collective-permute-done.19), kind=kLoop, calls=%fused_computation.20 | loop fusion | flops 2097152 | bytes 3145736 | tf_op jit(solution)/shard_map/convert_element_type | solution.py:126
  156.7 1.7 collective-permute-start.9
  158.4 8.6 %shard_map.97 = bf16[512,1024]{1,0:T(8,128)(2,1)} custom-call(s32[3]{0:T(128)} %get-tuple-element.21.place_ref, bf16[8,512,512]{2,1,0:T(8,128)(2,1)} %bitcast.90, bf16[8,512,512]{2,1,0:T(8,128)(2,1)} %bitcast.84, bf16[512,512]{1,0:T(8,128)(2,1)} %bitcast.103, bf16[512,512]{1,0:T(8,128)(2,1)} %copy-done.2, bf16[512,512]{1,0:T(8,128)(2,1)} %fusion.9.refs_4_, ...), custom_call_target="tpu_custom_call" | custom-call | flops 1 | bytes 1 | tf_op jit(solution)/shard_map/pallas_call | solution.py:215
  167.0 2.9 %add_convert_fusion = bf16[512,1024]{1,0:T(8,128)(2,1)} fusion(bf16[512,1024]{1,0:T(8,128)(2,1)} %collective-permute-done.29, bf16[512,1024]{1,0:T(8,128)(2,1)} %shard_map.97), kind=kLoop, calls=%fused_computation | loop fusion | flops 2097152 | bytes 3145728 | tf_op jit(solution)/shard_map/convert_element_type | solution.py:253
  169.9 5.0 %all-to-all-start = ((bf16[16,32,1024]{2,1,0:T(8,128)(2,1)}), bf16[16,32,1024]{2,1,0:T(8,128)(2,1)S(1)}, u32[]{:S(2)}, u32[]{:S(2)}) async-start(bf16[16,32,1024]{2,1,0:T(8,128)(2,1)} %bitcast.45), calls=%async_computation | async-start | bytes 2097152 | tf_op jit(solution)/shard_map/all_to_all | solution.py:254
  175.0 1.2 collective-permute-start.16
  176.2 1.5 collective-permute-start.20
  177.7 2.8 %fusion.14 = (bf16[512,512]{1,0:T(8,128)(2,1)}, bf16[512,512]{1,0:T(8,128)(2,1)}) fusion(bf16[512,512]{1,0:T(8,128)(2,1)} %collective-permute-done.9, bf16[8,512,512]{2,1,0:T(8,128)(2,1)} %bitcast.91, s32[]{:T(128)S(6)} %select_n.46, s32[]{:T(128)S(6)} %select_n.49, bf16[512,512]{1,0:T(8,128)(2,1)} %collective-permute-done.12), kind=kLoop, calls=%fused_computation.26 | loop fusion | flops 2097152 | bytes 3145736 | tf_op jit(solution)/shard_map/convert_element_type | solution.py:126
  180.5 7.5 %collective-permute-done.16 = bf16[512,512]{1,0:T(8,128)(2,1)} collective-permute-done((bf16[512,512]{1,0:T(8,128)(2,1)}, bf16[512,512]{1,0:T(8,128)(2,1)}, u32[]{:S(2)}, u32[]{:S(2)}) %collective-permute-start.16) | collective-permute-done | bytes 524320 | tf_op jit(solution)/shard_map/ppermute | solution.py:108
  188.1 2.8 %fusion.10 = (bf16[512,512]{1,0:T(8,128)(2,1)}, bf16[512,512]{1,0:T(8,128)(2,1)}) fusion(bf16[512,512]{1,0:T(8,128)(2,1)} %collective-permute-done.16, bf16[8,512,512]{2,1,0:T(8,128)(2,1)} %bitcast.85, s32[]{:T(128)S(6)} %select_n.46, s32[]{:T(128)S(6)} %select_n.49, bf16[512,512]{1,0:T(8,128)(2,1)} %collective-permute-done.20), kind=kLoop, calls=%fused_computation.18 | loop fusion | flops 2097152 | bytes 3145736 | tf_op jit(solution)/shard_map/convert_element_type | solution.py:126
  190.9 0.2 reduce_sum.24
  191.2 17.4 %all_to_all.15 = bf16[8,32,1024]{2,1,0:T(8,128)(2,1)S(1)} all-to-all(bf16[8,32,1024]{2,1,0:T(8,128)(2,1)S(1)} %broadcast_in_dim.7), channel_id=1, replica_groups=mesh['z'=8,'yh'=2,'x'=4,'yl'=2,'core'=2] {'z'}, dimensions={0} | all-to-all | bytes 1048576 | tf_op jit(solution)/shard_map/all_to_all | solution.py:257
  208.7 1.1 broadcast_in_dim.8
  209.8 5.9 %all-to-all-start.2 = ((bf16[16,32,1024]{2,1,0:T(8,128)(2,1)}), bf16[16,32,1024]{2,1,0:T(8,128)(2,1)S(1)}, u32[]{:S(2)}, u32[]{:S(2)}) async-start(bf16[16,32,1024]{2,1,0:T(8,128)(2,1)} %broadcast_in_dim.8), calls=%async_computation.2 | async-start | bytes 2097152 | tf_op jit(solution)/shard_map/all_to_all | solution.py:260
  215.8 2.7 %collective-permute-start.13 = (bf16[512,512]{1,0:T(8,128)(2,1)}, bf16[512,512]{1,0:T(8,128)(2,1)}, u32[]{:S(2)}, u32[]{:S(2)}) collective-permute-start(bf16[512,512]{1,0:T(8,128)(2,1)} %get-tuple-element.25), channel_id=1, source_target_pairs={{0,224},{32,0},{64,32},{96,64},{128,96},{160,128},{192,160},{224,1... | collective-permute-start | bytes 1572872 | tf_op jit(solution)/shard_map/ppermute | solution.py:108
  218.5 2.7 %collective-permute-start.21 = (bf16[512,512]{1,0:T(8,128)(2,1)}, bf16[512,512]{1,0:T(8,128)(2,1)}, u32[]{:S(2)}, u32[]{:S(2)}) collective-permute-start(bf16[512,512]{1,0:T(8,128)(2,1)} %get-tuple-element.29), channel_id=1, source_target_pairs={{0,224},{32,0},{64,32},{96,64},{128,96},{160,128},{192,160},{224,1... | collective-permute-start | bytes 1572872 | tf_op jit(solution)/shard_map/ppermute | solution.py:108
  221.1 1.9 constant_dynamic-slice_fusion.1
  223.0 5.1 %all-to-all-done.2 = bf16[16,32,1024]{2,1,0:T(8,128)(2,1)S(1)} async-done(((bf16[16,32,1024]{2,1,0:T(8,128)(2,1)}), bf16[16,32,1024]{2,1,0:T(8,128)(2,1)S(1)}, u32[]{:S(2)}, u32[]{:S(2)}) %all-to-all-start.2) | async-done | bytes 1048608 | tf_op jit(solution)/shard_map/all_to_all | solution.py:260
  228.2 6.7 %collective-permute-start.30 = (bf16[512,1024]{1,0:T(8,128)(2,1)S(1)}, bf16[512,1024]{1,0:T(8,128)(2,1)}, u32[]{:S(2)}, u32[]{:S(2)}) collective-permute-start(bf16[512,1024]{1,0:T(8,128)(2,1)S(1)} %bitcast.98), channel_id=1, source_target_pairs={{0,1},{1,0},{2,3},{3,2},{4,5},{5,4},{6,7},{7,6},{8,9},{9,8},{10,11... | collective-permute-start | bytes 3145736 | tf_op jit(solution)/shard_map/ppermute | solution.py:108
  234.9 1.9 fusion.22
  236.8 0.5 collective-permute-start.14
  237.3 1.1 constant_dynamic-slice_fusion
  238.4 0.8 copy-done.8
  239.2 1.8 fusion.23
  241.0 2.5 collective-permute-start.22
  243.5 0.3 collective-permute-done.14
  243.8 1.2 fusion.21
  245.0 4.5 %collective-permute-done.22 = bf16[256,512]{1,0:T(8,128)(2,1)} collective-permute-done((bf16[256,512]{1,0:T(8,128)(2,1)}, bf16[256,512]{1,0:T(8,128)(2,1)}, u32[]{:S(2)}, u32[]{:S(2)}) %collective-permute-start.22) | collective-permute-done | bytes 262176 | tf_op jit(solution)/shard_map/ppermute | solution.py:108
  249.5 1.3 fusion.20
  250.8 1.6 fusion
  252.4 4.7 %shard_map.98 = f32[1024,1024]{1,0:T(8,128)} custom-call(s32[1]{0:T(128)} %bitcast.41.core_ref, bf16[512,1024]{1,0:T(8,128)(2,1)} %bitcast.99, bf16[512,1024]{1,0:T(8,128)(2,1)} %collective-permute-done.30.other_ref), custom_call_target="tpu_custom_call" | custom-call | tf_op jit(solution)/shard_map/pallas_call | solution.py:240
  (50 shorter events, 0.6 us)
Async XLA Ops:
  7.2 243.7 %copy-start = (bf16[1024,1024]{1,0:T(8,128)(2,1)S(1)}, bf16[1024,1024]{1,0:T(8,128)(2,1)}, u32[]{:S(2)}) copy-start(bf16[1024,1024]{1,0:T(8,128)(2,1)} %param.11) | copy-start | bytes 6291460
  7.2 67.4 %all-gather.2.cloned.1.call-start = ((), (), s32[]{:S(2)}) async-start(), calls=%async_computation.3 | async-start | bytes 8912896 | tf_op jit(solution)/shard_map/all_gather | solution.py:272
  11.1 80.7 %copy-start.1 = (bf16[1,256,1024]{1,2,0:T(8,128)(2,1)}, bf16[1,256,1024]{1,2,0:T(8,128)(2,1)S(1)}, u32[]{:S(2)}) copy-start(bf16[1,256,1024]{1,2,0:T(8,128)(2,1)S(1)} %copy.11) | copy-start | bytes 1572868
  11.1 17.1 %collective-permute-start.1 = (bf16[1024,256]{1,0:T(8,128)(2,1)S(1)}, bf16[1024,256]{1,0:T(8,128)(2,1)S(1)}, u32[]{:S(2)}, u32[]{:S(2)}) collective-permute-start(bf16[1024,256]{1,0:T(8,128)(2,1)S(1)} %bitcast.93), channel_id=1, source_target_pairs={{0,224},{32,0},{64,32},{96,64},{128,96},{160,128},{192,160},{224,1... | collective-permute-start | bytes 1572872 | tf_op jit(solution)/shard_map/ppermute | solution.py:108
  17.6 13.8 %collective-permute-start.2 = (bf16[1024,256]{1,0:T(8,128)(2,1)S(1)}, bf16[1024,256]{1,0:T(8,128)(2,1)}, u32[]{:S(2)}, u32[]{:S(2)}) collective-permute-start(bf16[1024,256]{1,0:T(8,128)(2,1)S(1)} %bitcast.94), channel_id=1, source_target_pairs={{0,32},{32,64},{64,96},{96,128},{128,160},{160,192},{192,224},{224... | collective-permute-start | bytes 1572872 | tf_op jit(solution)/shard_map/ppermute | solution.py:108
  17.6 17.7 %collective-permute-start = (bf16[1024,256]{1,0:T(8,128)(2,1)S(1)}, bf16[1024,256]{1,0:T(8,128)(2,1)S(1)}, u32[]{:S(2)}, u32[]{:S(2)}) collective-permute-start(bf16[1024,256]{1,0:T(8,128)(2,1)S(1)} %bitcast.95), channel_id=1, source_target_pairs={{0,16},{16,0},{1,17},{17,1},{2,18},{18,2},{3,19},{19,3},{4,20},{20... | collective-permute-start | bytes 1572872 | tf_op jit(solution)/shard_map/ppermute | solution.py:108
  28.2 63.6 %copy-start.5 = (bf16[1024,256]{1,0:T(8,128)(2,1)}, bf16[1024,256]{1,0:T(8,128)(2,1)S(1)}, u32[]{:S(2)}) copy-start(bf16[1024,256]{1,0:T(8,128)(2,1)S(1)} %collective-permute-done.1.refs_10_) | copy-start | bytes 1572868
  35.2 1.6 copy-start.6
  35.2 8.7 %collective-permute-start.3 = (bf16[1024,256]{1,0:T(8,128)(2,1)S(1)}, bf16[1024,256]{1,0:T(8,128)(2,1)}, u32[]{:S(2)}, u32[]{:S(2)}) collective-permute-start(bf16[1024,256]{1,0:T(8,128)(2,1)S(1)} %collective-permute-done.refs_16_), channel_id=1, source_target_pairs={{0,224},{32,0},{64,32},{96,64},{128,96},{160,128},{192,160},{224,1... | collective-permute-start | bytes 1572872 | tf_op jit(solution)/shard_map/ppermute | solution.py:108
  36.9 9.3 %collective-permute-start.5 = (bf16[1024,256]{1,0:T(8,128)(2,1)S(1)}, bf16[1024,256]{1,0:T(8,128)(2,1)}, u32[]{:S(2)}, u32[]{:S(2)}) collective-permute-start(bf16[1024,256]{1,0:T(8,128)(2,1)S(1)} %collective-permute-done.refs_16_), channel_id=1, source_target_pairs={{0,32},{32,64},{64,96},{96,128},{128,160},{160,192},{192,224},{224... | collective-permute-start | bytes 1572872 | tf_op jit(solution)/shard_map/ppermute | solution.py:108
  44.0 10.9 %collective-permute-start.4 = (bf16[1024,256]{1,0:T(8,128)(2,1)}, bf16[1024,256]{1,0:T(8,128)(2,1)}, u32[]{:S(2)}, u32[]{:S(2)}) collective-permute-start(bf16[1024,256]{1,0:T(8,128)(2,1)} %collective-permute-done.3.refs_17_), channel_id=1, source_target_pairs={{0,224},{32,0},{64,32},{96,64},{128,96},{160,128},{192,160},{224,1... | collective-permute-start | bytes 1572872 | tf_op jit(solution)/shard_map/ppermute | solution.py:108
  46.2 12.1 %collective-permute-start.6 = (bf16[1024,256]{1,0:T(8,128)(2,1)}, bf16[1024,256]{1,0:T(8,128)(2,1)}, u32[]{:S(2)}, u32[]{:S(2)}) collective-permute-start(bf16[1024,256]{1,0:T(8,128)(2,1)} %collective-permute-done.5.refs_15_), channel_id=1, source_target_pairs={{0,32},{32,64},{64,96},{96,128},{128,160},{160,192},{192,224},{224... | collective-permute-start | bytes 1572872 | tf_op jit(solution)/shard_map/ppermute | solution.py:108
  46.2 45.6 %collective-permute-start.23 = (bf16[1024,256]{1,0:T(8,128)(2,1)}, bf16[1024,256]{1,0:T(8,128)(2,1)}, u32[]{:S(2)}, u32[]{:S(2)}) collective-permute-start(bf16[1024,256]{1,0:T(8,128)(2,1)} %collective-permute-done.2.refs_8_), channel_id=1, source_target_pairs={{0,32},{32,64},{64,96},{96,128},{128,160},{160,192},{192,224},{224... | collective-permute-start | bytes 1572872 | tf_op jit(solution)/shard_map/ppermute | solution.py:108
  47.5 47.1 %collective-permute-start.25 = (bf16[1024,256]{1,0:T(8,128)(2,1)S(1)}, bf16[1024,256]{1,0:T(8,128)(2,1)}, u32[]{:S(2)}, u32[]{:S(2)}) collective-permute-start(bf16[1024,256]{1,0:T(8,128)(2,1)S(1)} %collective-permute-done.1.refs_10_), channel_id=1, source_target_pairs={{0,224},{32,0},{64,32},{96,64},{128,96},{160,128},{192,160},{224,1... | collective-permute-start | bytes 1572872 | tf_op jit(solution)/shard_map/ppermute | solution.py:108
  91.8 15.5 %collective-permute-start.7 = (bf16[512,512]{1,0:T(8,128)(2,1)}, bf16[512,512]{1,0:T(8,128)(2,1)}, u32[]{:S(2)}, u32[]{:S(2)}) collective-permute-start(bf16[512,512]{1,0:T(8,128)(2,1)} %bitcast.111), channel_id=1, source_target_pairs={{0,32},{32,64},{64,96},{96,128},{128,160},{160,192},{192,224},{224... | collective-permute-start | bytes 1572872 | tf_op jit(solution)/shard_map/ppermute | solution.py:108
  91.9 26.7 %collective-permute-start.24 = (bf16[1024,256]{1,0:T(8,128)(2,1)}, bf16[1024,256]{1,0:T(8,128)(2,1)S(1)}, u32[]{:S(2)}, u32[]{:S(2)}) collective-permute-start(bf16[1024,256]{1,0:T(8,128)(2,1)} %collective-permute-done.23.refs_7_), channel_id=1, source_target_pairs={{0,32},{32,64},{64,96},{96,128},{128,160},{160,192},{192,224},{224... | collective-permute-start | bytes 1572872 | tf_op jit(solution)/shard_map/ppermute | solution.py:108
  91.9 26.7 %collective-permute-start.18 = (bf16[512,512]{1,0:T(8,128)(2,1)}, bf16[512,512]{1,0:T(8,128)(2,1)}, u32[]{:S(2)}, u32[]{:S(2)}) collective-permute-start(bf16[512,512]{1,0:T(8,128)(2,1)} %bitcast.110), channel_id=1, source_target_pairs={{0,224},{32,0},{64,32},{96,64},{128,96},{160,128},{192,160},{224,1... | collective-permute-start | bytes 1572872 | tf_op jit(solution)/shard_map/ppermute | solution.py:108
  94.6 27.6 %collective-permute-start.26 = (bf16[1024,256]{1,0:T(8,128)(2,1)}, bf16[1024,256]{1,0:T(8,128)(2,1)}, u32[]{:S(2)}, u32[]{:S(2)}) collective-permute-start(bf16[1024,256]{1,0:T(8,128)(2,1)} %collective-permute-done.25.refs_11_), channel_id=1, source_target_pairs={{0,224},{32,0},{64,32},{96,64},{128,96},{160,128},{192,160},{224,1... | collective-permute-start | bytes 1572872 | tf_op jit(solution)/shard_map/ppermute | solution.py:108
  96.0 32.5 %collective-permute-start.27 = (bf16[1024,256]{1,0:T(8,128)(2,1)}, bf16[1024,256]{1,0:T(8,128)(2,1)}, u32[]{:S(2)}, u32[]{:S(2)}) collective-permute-start(bf16[1024,256]{1,0:T(8,128)(2,1)} %collective-permute-done.6.refs_14_), channel_id=1, source_target_pairs={{0,32},{32,64},{64,96},{96,128},{128,160},{160,192},{192,224},{224... | collective-permute-start | bytes 1572872 | tf_op jit(solution)/shard_map/ppermute | solution.py:108
  107.3 21.9 %collective-permute-start.28 = (bf16[1024,256]{1,0:T(8,128)(2,1)}, bf16[1024,256]{1,0:T(8,128)(2,1)}, u32[]{:S(2)}, u32[]{:S(2)}) collective-permute-start(bf16[1024,256]{1,0:T(8,128)(2,1)} %collective-permute-done.4.refs_18_), channel_id=1, source_target_pairs={{0,224},{32,0},{64,32},{96,64},{128,96},{160,128},{192,160},{224,1... | collective-permute-start | bytes 1572872 | tf_op jit(solution)/shard_map/ppermute | solution.py:108
  109.3 19.9 %copy-start.2 = (bf16[512,512]{1,0:T(8,128)(2,1)}, bf16[512,512]{1,0:T(8,128)(2,1)S(1)}, u32[]{:S(2)}) copy-start(bf16[512,512]{1,0:T(8,128)(2,1)S(1)} %fusion.16.refs_3_) | copy-start | bytes 1572868
  118.6 10.6 %copy-start.7 = (bf16[1024,256]{1,0:T(8,128)(2,1)}, bf16[1024,256]{1,0:T(8,128)(2,1)S(1)}, u32[]{:S(2)}) copy-start(bf16[1024,256]{1,0:T(8,128)(2,1)S(1)} %collective-permute-done.24.refs_6_) | copy-start | bytes 1572868
  118.6 23.1 %collective-permute-start.11 = (bf16[512,512]{1,0:T(8,128)(2,1)}, bf16[512,512]{1,0:T(8,128)(2,1)}, u32[]{:S(2)}, u32[]{:S(2)}) collective-permute-start(bf16[512,512]{1,0:T(8,128)(2,1)} %bitcast.101), channel_id=1, source_target_pairs={{0,224},{32,0},{64,32},{96,64},{128,96},{160,128},{192,160},{224,1... | collective-permute-start | bytes 1572872 | tf_op jit(solution)/shard_map/ppermute | solution.py:108
  118.6 23.1 %collective-permute-start.8 = (bf16[512,512]{1,0:T(8,128)(2,1)S(1)}, bf16[512,512]{1,0:T(8,128)(2,1)}, u32[]{:S(2)}, u32[]{:S(2)}) collective-permute-start(bf16[512,512]{1,0:T(8,128)(2,1)S(1)} %fusion.16.refs_3_), channel_id=1, source_target_pairs={{0,32},{32,64},{64,96},{96,128},{128,160},{160,192},{192,224},{224... | collective-permute-start | bytes 1572872 | tf_op jit(solution)/shard_map/ppermute | solution.py:108
  129.2 9.2 %copy-start.3 = (bf16[512,512]{1,0:T(8,128)(2,1)S(1)}, bf16[512,512]{1,0:T(8,128)(2,1)}, u32[]{:S(2)}) copy-start(bf16[512,512]{1,0:T(8,128)(2,1)} %fusion.9.refs_4_) | copy-start | bytes 1572868
  138.0 29.0 %collective-permute-start.29 = (bf16[512,1024]{1,0:T(8,128)(2,1)}, bf16[512,1024]{1,0:T(8,128)(2,1)}, u32[]{:S(2)}, u32[]{:S(2)}) collective-permute-start(bf16[512,1024]{1,0:T(8,128)(2,1)} %shard_map.96), channel_id=1, source_target_pairs={{0,1},{1,0},{2,3},{3,2},{4,5},{5,4},{6,7},{7,6},{8,9},{9,8},{10,11... | collective-permute-start | bytes 3145736 | tf_op jit(solution)/shard_map/ppermute | solution.py:108
  138.5 15.4 %collective-permute-start.15 = (bf16[512,512]{1,0:T(8,128)(2,1)}, bf16[512,512]{1,0:T(8,128)(2,1)}, u32[]{:S(2)}, u32[]{:S(2)}) collective-permute-start(bf16[512,512]{1,0:T(8,128)(2,1)} %bitcast.27.refs_5_), channel_id=1, source_target_pairs={{0,32},{32,64},{64,96},{96,128},{128,160},{160,192},{192,224},{224... | collective-permute-start | bytes 1572872 | tf_op jit(solution)/shard_map/ppermute | solution.py:108
  138.5 15.5 %collective-permute-start.19 = (bf16[512,512]{1,0:T(8,128)(2,1)S(1)}, bf16[512,512]{1,0:T(8,128)(2,1)}, u32[]{:S(2)}, u32[]{:S(2)}) collective-permute-start(bf16[512,512]{1,0:T(8,128)(2,1)S(1)} %copy-done.3), channel_id=1, source_target_pairs={{0,224},{32,0},{64,32},{96,64},{128,96},{160,128},{192,160},{224,1... | collective-permute-start | bytes 1572872 | tf_op jit(solution)/shard_map/ppermute | solution.py:108
  144.5 33.2 %collective-permute-start.12 = (bf16[512,512]{1,0:T(8,128)(2,1)}, bf16[512,512]{1,0:T(8,128)(2,1)}, u32[]{:S(2)}, u32[]{:S(2)}) collective-permute-start(bf16[512,512]{1,0:T(8,128)(2,1)} %get-tuple-element.27), channel_id=1, source_target_pairs={{0,224},{32,0},{64,32},{96,64},{128,96},{160,128},{192,160},{224,1... | collective-permute-start | bytes 1572872 | tf_op jit(solution)/shard_map/ppermute | solution.py:108
  156.7 21.0 %collective-permute-start.9 = (bf16[512,512]{1,0:T(8,128)(2,1)}, bf16[512,512]{1,0:T(8,128)(2,1)}, u32[]{:S(2)}, u32[]{:S(2)}) collective-permute-start(bf16[512,512]{1,0:T(8,128)(2,1)} %get-tuple-element.26), channel_id=1, source_target_pairs={{0,32},{32,64},{64,96},{96,128},{128,160},{160,192},{192,224},{224... | collective-permute-start | bytes 1572872 | tf_op jit(solution)/shard_map/ppermute | solution.py:108
  169.9 21.0 %all-to-all-start = ((bf16[16,32,1024]{2,1,0:T(8,128)(2,1)}), bf16[16,32,1024]{2,1,0:T(8,128)(2,1)S(1)}, u32[]{:S(2)}, u32[]{:S(2)}) async-start(bf16[16,32,1024]{2,1,0:T(8,128)(2,1)} %bitcast.45), calls=%async_computation | async-start | bytes 2097152 | tf_op jit(solution)/shard_map/all_to_all | solution.py:254
  175.0 13.1 %collective-permute-start.16 = (bf16[512,512]{1,0:T(8,128)(2,1)}, bf16[512,512]{1,0:T(8,128)(2,1)}, u32[]{:S(2)}, u32[]{:S(2)}) collective-permute-start(bf16[512,512]{1,0:T(8,128)(2,1)} %get-tuple-element.30), channel_id=1, source_target_pairs={{0,32},{32,64},{64,96},{96,128},{128,160},{160,192},{192,224},{224... | collective-permute-start | bytes 1572872 | tf_op jit(solution)/shard_map/ppermute | solution.py:108
  176.2 11.9 %collective-permute-start.20 = (bf16[512,512]{1,0:T(8,128)(2,1)}, bf16[512,512]{1,0:T(8,128)(2,1)}, u32[]{:S(2)}, u32[]{:S(2)}) collective-permute-start(bf16[512,512]{1,0:T(8,128)(2,1)} %get-tuple-element.31), channel_id=1, source_target_pairs={{0,224},{32,0},{64,32},{96,64},{128,96},{160,128},{192,160},{224,1... | collective-permute-start | bytes 1572872 | tf_op jit(solution)/shard_map/ppermute | solution.py:108
  209.8 18.3 %all-to-all-start.2 = ((bf16[16,32,1024]{2,1,0:T(8,128)(2,1)}), bf16[16,32,1024]{2,1,0:T(8,128)(2,1)S(1)}, u32[]{:S(2)}, u32[]{:S(2)}) async-start(bf16[16,32,1024]{2,1,0:T(8,128)(2,1)} %broadcast_in_dim.8), calls=%async_computation.2 | async-start | bytes 2097152 | tf_op jit(solution)/shard_map/all_to_all | solution.py:260
  215.7 19.2 %collective-permute-start.10 = (bf16[512,512]{1,0:T(8,128)(2,1)}, bf16[512,512]{1,0:T(8,128)(2,1)}, u32[]{:S(2)}, u32[]{:S(2)}) collective-permute-start(bf16[512,512]{1,0:T(8,128)(2,1)} %get-tuple-element.24), channel_id=1, source_target_pairs={{0,32},{32,64},{64,96},{96,128},{128,160},{160,192},{192,224},{224... | collective-permute-start | bytes 1572872 | tf_op jit(solution)/shard_map/ppermute | solution.py:108
  215.8 19.1 %collective-permute-start.13 = (bf16[512,512]{1,0:T(8,128)(2,1)}, bf16[512,512]{1,0:T(8,128)(2,1)}, u32[]{:S(2)}, u32[]{:S(2)}) collective-permute-start(bf16[512,512]{1,0:T(8,128)(2,1)} %get-tuple-element.25), channel_id=1, source_target_pairs={{0,224},{32,0},{64,32},{96,64},{128,96},{160,128},{192,160},{224,1... | collective-permute-start | bytes 1572872 | tf_op jit(solution)/shard_map/ppermute | solution.py:108
  218.5 19.9 %collective-permute-start.17 = (bf16[512,512]{1,0:T(8,128)(2,1)}, bf16[512,512]{1,0:T(8,128)(2,1)}, u32[]{:S(2)}, u32[]{:S(2)}) collective-permute-start(bf16[512,512]{1,0:T(8,128)(2,1)} %get-tuple-element.28), channel_id=1, source_target_pairs={{0,32},{32,64},{64,96},{96,128},{128,160},{160,192},{192,224},{224... | collective-permute-start | bytes 1572872 | tf_op jit(solution)/shard_map/ppermute | solution.py:108
  218.5 20.0 %collective-permute-start.21 = (bf16[512,512]{1,0:T(8,128)(2,1)}, bf16[512,512]{1,0:T(8,128)(2,1)}, u32[]{:S(2)}, u32[]{:S(2)}) collective-permute-start(bf16[512,512]{1,0:T(8,128)(2,1)} %get-tuple-element.29), channel_id=1, source_target_pairs={{0,224},{32,0},{64,32},{96,64},{128,96},{160,128},{192,160},{224,1... | collective-permute-start | bytes 1572872 | tf_op jit(solution)/shard_map/ppermute | solution.py:108
  228.1 24.3 %copy-start.4 = (bf16[16,32,1024]{2,1,0:T(8,128)(2,1)}, bf16[16,32,1024]{2,1,0:T(8,128)(2,1)S(1)}, u32[]{:S(2)}) copy-start(bf16[16,32,1024]{2,1,0:T(8,128)(2,1)S(1)} %all-to-all-done.2) | copy-start | bytes 3145732
  228.2 24.3 %collective-permute-start.30 = (bf16[512,1024]{1,0:T(8,128)(2,1)S(1)}, bf16[512,1024]{1,0:T(8,128)(2,1)}, u32[]{:S(2)}, u32[]{:S(2)}) collective-permute-start(bf16[512,1024]{1,0:T(8,128)(2,1)S(1)} %bitcast.98), channel_id=1, source_target_pairs={{0,1},{1,0},{2,3},{3,2},{4,5},{5,4},{6,7},{7,6},{8,9},{9,8},{10,11... | collective-permute-start | bytes 3145736 | tf_op jit(solution)/shard_map/ppermute | solution.py:108
  236.8 6.9 %collective-permute-start.14 = (bf16[256,512]{1,0:T(8,128)(2,1)}, bf16[256,512]{1,0:T(8,128)(2,1)S(1)}, u32[]{:S(2)}, u32[]{:S(2)}) collective-permute-start(bf16[256,512]{1,0:T(8,128)(2,1)} %fusion.22), channel_id=1, source_target_pairs={{0,16},{16,0},{1,17},{17,1},{2,18},{18,2},{3,19},{19,3},{4,20},{20... | collective-permute-start | bytes 786440 | tf_op jit(solution)/shard_map/ppermute | solution.py:108
  238.4 0.8 copy-start.8
  241.0 8.5 %collective-permute-start.22 = (bf16[256,512]{1,0:T(8,128)(2,1)}, bf16[256,512]{1,0:T(8,128)(2,1)}, u32[]{:S(2)}, u32[]{:S(2)}) collective-permute-start(bf16[256,512]{1,0:T(8,128)(2,1)} %fusion.23), channel_id=1, source_target_pairs={{0,16},{16,0},{1,17},{17,1},{2,18},{18,2},{3,19},{19,3},{4,20},{20... | collective-permute-start | bytes 786440 | tf_op jit(solution)/shard_map/ppermute | solution.py:108
Sparse Core Ops, SparseCore 0:
  10.4 64.0 all-gather.1
